TPU v7x, 128 devices: a whole 4x4x4 slice. The times are simulated.
128 devices in a mesh: row: 4 (over x), col: 32 (over y, z, core).
Axes of the slice: x: 4, y: 4, z: 4, core: 2. Of those that a mesh axis runs over, the one named last changes fastest.
Arguments:
- pair_slab: bfloat16 [32, 4096, 128], P('row', 'col'), may hold values from -6 to 6
- pair_bias: bfloat16 [4, 4096, 4096], P(None, 'col', 'row'), may hold values from -5 to 240
- tile_mask: int32 [64, 64], replicated, may hold values from 0 to 1, as said below
- w_proj: bfloat16 [128, 512], replicated, may hold values from -0.5 to 0.5
- w_out: bfloat16 [128, 128], replicated, may hold values from -0.5 to 0.5
- d_out: bfloat16 [32, 4096, 128], P('row', 'col'), may hold values from -6 to 6
Outputs:
- attn_out: bfloat16 [32, 4096, 128], P('row', 'col')
- slab_grads: bfloat16 [32, 4096, 128], P('row', 'col')
- bias_grads: float32 [4096, 4, 4096], P(('row', 'col'))
Inputs may be any that keep to these rules, and one draw needn't show every extreme that they name: tile_mask[a, a] is 1 for every tile a, and tile_mask[a, b] is 0 wherever b > a.
All inputs are finite; a program needn't handle non-finite values.
Results may differ from a plain program's by a relative error of at most 0.019.
Values may be sent and summed in bfloat16 or wider, within the bound.
A program may use at most 192 MiB of HBM per device.

v0:
```python
import jax
import jax.numpy as jnp
from jax import lax
from jax.sharding import PartitionSpec as P

H = 4
DH = 32
TILE = 64


eps_norm = 1e-05
neg_big = -1e30


def normalize(pair_slab):
    entries = pair_slab.astype(jnp.float32)
    centred = entries - jnp.mean(entries, axis=-1, keepdims=True)
    spread = jnp.mean(centred * centred, axis=-1, keepdims=True)
    return centred * lax.rsqrt(spread + eps_norm)


def expand_tiles(tile_block):
    grown = jnp.repeat(jnp.repeat(tile_block, TILE, axis=0), TILE, axis=1)
    return (grown > 0)[None, None]


def pair_scores(query_heads, key_heads, bias_block):
    scores = jnp.einsum(
        "rjhd,rkhd->rhjk", query_heads, key_heads, preferred_element_type=jnp.float32
    )
    return scores + bias_block[None].astype(jnp.float32)


def on_device(pair_slab, pair_bias, tile_mask, w_proj, w_out, d_out):
    row_count, col_count, channels = pair_slab.shape
    head_width = H * DH
    q_scale = DH ** (-0.5)
    own_start = lax.axis_index("col") * col_count
    normed_f, norm_pull = jax.vjp(normalize, pair_slab)
    normed = normed_f.astype(jnp.bfloat16)
    flat_normed = normed.reshape(row_count * col_count, channels)
    w_query = w_proj[:, :head_width]
    w_pair = w_proj[:, head_width : 3 * head_width]
    w_gate = w_proj[:, 3 * head_width :]
    w_pair_back = jnp.transpose(w_pair).astype(jnp.float32)
    queries = (jnp.dot(flat_normed, w_query, preferred_element_type=jnp.float32) * q_scale).astype(
        jnp.bfloat16
    )
    query_heads = queries.reshape(row_count, col_count, H, DH)
    gating = jax.nn.sigmoid(jnp.dot(flat_normed, w_gate, preferred_element_type=jnp.float32))
    gating = gating.reshape(row_count, col_count, head_width)
    bias_rows = lax.all_gather(pair_bias, "row", axis=2, tiled=True)
    gathered_slab = lax.all_gather(normed, "col", axis=1, tiled=True)
    key_values = jnp.dot(
        gathered_slab.reshape(-1, channels), w_pair, preferred_element_type=jnp.float32
    )
    key_values = key_values.astype(jnp.bfloat16).reshape(row_count, -1, 2 * head_width)
    total_cols = key_values.shape[1]
    block_len = min(512, total_cols)
    block_count = total_cols // block_len
    block_ids = jnp.arange(block_count, dtype=jnp.int32)

    def key_slices(block_index):
        key_start = block_index * block_len
        chosen = lax.dynamic_slice_in_dim(key_values, key_start, block_len, 1)
        key_heads = chosen[..., :head_width].reshape(row_count, block_len, H, DH)
        value_heads = chosen[..., head_width:].reshape(row_count, block_len, H, DH)
        bias_block = lax.dynamic_slice_in_dim(bias_rows, key_start, block_len, 2)
        tile_block = lax.dynamic_slice(
            tile_mask,
            (own_start // TILE, key_start // TILE),
            (col_count // TILE, block_len // TILE),
        )
        return (key_heads, value_heads, bias_block, tile_block)

    def stats_step(carried, block_index):
        key_heads, value_heads, bias_block, tile_block = key_slices(block_index)

        def stats_live(running):
            running_max, running_sum = running
            active = expand_tiles(tile_block)
            scores = jnp.where(active, pair_scores(query_heads, key_heads, bias_block), neg_big)
            new_max = jnp.maximum(running_max, jnp.max(scores, axis=-1))
            exp_terms = jnp.where(active, jnp.exp(scores - new_max[..., None]), 0.0)
            return (
                new_max,
                running_sum * jnp.exp(running_max - new_max) + jnp.sum(exp_terms, axis=-1),
            )

        return (
            lax.cond(jnp.any(tile_block > 0), stats_live, lambda unchanged: unchanged, carried),
            None,
        )

    start_max = jnp.full((row_count, H, col_count), neg_big, jnp.float32)
    start_sum = jnp.zeros((row_count, H, col_count), jnp.float32)
    (top_score, exp_total), _ = lax.scan(stats_step, (start_max, start_sum), block_ids)
    log_norm = top_score + jnp.log(exp_total)

    def value_step(carried, block_index):
        key_heads, value_heads, bias_block, tile_block = key_slices(block_index)

        def value_live(value_acc):
            active = expand_tiles(tile_block)
            scores = pair_scores(query_heads, key_heads, bias_block)
            weights = jnp.where(active, jnp.exp(scores - log_norm[..., None]), 0.0).astype(
                jnp.bfloat16
            )
            return value_acc + jnp.einsum(
                "rhjk,rkhd->rjhd", weights, value_heads, preferred_element_type=jnp.float32
            )

        return (
            lax.cond(jnp.any(tile_block > 0), value_live, lambda unchanged: unchanged, carried),
            None,
        )

    value_acc, _ = lax.scan(
        value_step, jnp.zeros((row_count, col_count, H, DH), jnp.float32), block_ids
    )
    attended = value_acc.reshape(row_count, col_count, head_width)
    gated = (gating * attended).astype(jnp.bfloat16)
    attn_out = jnp.dot(gated.reshape(-1, head_width), w_out, preferred_element_type=jnp.float32)
    attn_out = attn_out.astype(jnp.bfloat16).reshape(row_count, col_count, channels)
    d_gated = jnp.dot(
        d_out.reshape(-1, channels), jnp.transpose(w_out), preferred_element_type=jnp.float32
    )
    d_gated = d_gated.reshape(row_count, col_count, head_width)
    d_attended = (d_gated * gating).astype(jnp.bfloat16)
    d_gate_lin = d_gated * attended * gating * (1.0 - gating)
    row_delta = jnp.sum(
        (d_attended.astype(jnp.float32) * attended).reshape(row_count, col_count, H, DH), axis=-1
    )
    row_delta = jnp.transpose(row_delta, (0, 2, 1))
    d_att_heads = d_attended.reshape(row_count, col_count, H, DH)

    def grad_step(carried, block_index):
        key_heads, value_heads, bias_block, tile_block = key_slices(block_index)

        def grad_live(d_query_acc):
            active = expand_tiles(tile_block)
            scores = pair_scores(query_heads, key_heads, bias_block)
            probs = jnp.where(active, jnp.exp(scores - log_norm[..., None]), 0.0)
            weights = probs.astype(jnp.bfloat16)
            d_probs = jnp.einsum(
                "rjhd,rkhd->rhjk", d_att_heads, value_heads, preferred_element_type=jnp.float32
            )
            d_scores = probs * (d_probs - row_delta[..., None])
            d_scores_b = d_scores.astype(jnp.bfloat16)
            d_query_acc = d_query_acc + jnp.einsum(
                "rhjk,rkhd->rjhd", d_scores_b, key_heads, preferred_element_type=jnp.float32
            )
            bias_term = jnp.einsum("rhjk->khj", d_scores)
            d_keys = jnp.einsum(
                "rhjk,rjhd->krhd", d_scores_b, query_heads, preferred_element_type=jnp.float32
            )
            d_values = jnp.einsum(
                "rhjk,rjhd->krhd", weights, d_att_heads, preferred_element_type=jnp.float32
            )
            pair_term = jnp.concatenate(
                [
                    d_keys.reshape(block_len, row_count, head_width),
                    d_values.reshape(block_len, row_count, head_width),
                ],
                axis=-1,
            )
            pair_term = jnp.dot(
                pair_term.reshape(block_len * row_count, 2 * head_width),
                w_pair_back,
                precision=lax.Precision.HIGHEST,
            )
            pair_term = pair_term.reshape(block_len, row_count, channels)
            return (d_query_acc, (bias_term, pair_term))

        def skipped(d_query_acc):
            bias_zero = jnp.zeros((block_len, H, col_count), jnp.float32)
            pair_zero = jnp.zeros((block_len, row_count, channels), jnp.float32)
            return (d_query_acc, (bias_zero, pair_zero))

        return lax.cond(jnp.any(tile_block > 0), grad_live, skipped, carried)

    d_query_acc, block_terms = lax.scan(
        grad_step, jnp.zeros((row_count, col_count, H, DH), jnp.float32), block_ids
    )
    bias_terms = block_terms[0].reshape(total_cols, H, col_count)
    pair_terms = block_terms[1].reshape(total_cols, row_count, channels)
    pair_sum = lax.psum_scatter(
        pair_terms.astype(jnp.bfloat16), "col", scatter_dimension=0, tiled=True
    ).astype(jnp.float32)
    pair_back = jnp.transpose(pair_sum, (1, 0, 2)).reshape(-1, channels)
    d_qg = jnp.concatenate(
        [
            d_query_acc.reshape(row_count * col_count, head_width) * q_scale,
            d_gate_lin.reshape(row_count * col_count, head_width),
        ],
        axis=-1,
    ).astype(jnp.bfloat16)
    w_qg_back = jnp.transpose(jnp.concatenate([w_query, w_gate], axis=1))
    d_normed = jnp.dot(d_qg, w_qg_back, preferred_element_type=jnp.float32) + pair_back
    slab_grads = norm_pull(d_normed.reshape(row_count, col_count, channels))[0]
    partial_sum = lax.psum_scatter(
        bias_terms.astype(jnp.bfloat16), "row", scatter_dimension=0, tiled=True
    ).astype(jnp.float32)
    bias_grads = lax.all_to_all(
        partial_sum.astype(jnp.bfloat16), "col", split_axis=0, concat_axis=2, tiled=True
    ).astype(partial_sum.dtype)
    return (attn_out, slab_grads, bias_grads)


def solution(mesh):
    in_specs = (P("row", "col", None), P(None, "col", "row"), P(), P(), P(), P("row", "col", None))
    out_specs = (P("row", "col", None), P("row", "col", None), P(("row", "col"), None, None))
    return jax.shard_map(
        on_device, mesh=mesh, in_specs=in_specs, out_specs=out_specs, check_vma=False
    )
```

profile of v0, /device:TPU:1, one launch (start us, length us, event | category | flops | bytes accessed | tf_op | source)
XLA Modules:
  0.0 813.0 jit_solution(17003910610374804841)
XLA Ops:
  10.9 2.0 fusion.54
  13.0 2.3 copy.97
  21.4 48.5 %all-gather.3.cloned.1.call-done = bf16[8,4096,128]{2,1,0:T(8,128)(2,1)} async-done(((bf16[8,128,128]{2,1,0:T(8,128)(2,1)}), bf16[8,4096,128]{2,1,0:T(8,128)(2,1)}) %all-gather.3.cloned.1.call-update) | async-done | bytes 8388624 | tf_op jit(solution)/shard_map/all_gather | solution.py:53
  69.8 14.5 %convolution_convert_fusion = bf16[32768,256]{1,0:T(8,128)(2,1)} fusion(bf16[32768,128]{1,0:T(8,128)(2,1)} %bitcast.185, bf16[128,512]{1,0:T(8,128)(2,1)S(1)} %copy-done.10), kind=kOutput, calls=%fused_computation.54 | convolution fusion | flops 2155872256 | bytes 25231360 | tf_op jit(solution)/shard_map/dot_general | solution.py:54
  84.3 21.2 %copy.102 = bf16[8,4096,256]{1,2,0:T(8,128)(2,1)} copy(bf16[8,4096,256]{2,1,0:T(8,128)(2,1)} %bitcast.178) | data formatting | bytes 33554432 | tf_op jit(solution)/shard_map/while | solution.py:118
  105.5 13.9 %all-gather.5.cloned.1.call-done = bf16[4,128,4096]{1,2,0:T(8,128)(2,1)} async-done(((bf16[4,128,1024]{1,2,0:T(8,128)(2,1)}), bf16[4,128,4096]{1,2,0:T(8,128)(2,1)}) %all-gather.5.cloned.1.call-update) | async-done | bytes 4194320 | tf_op jit(solution)/shard_map/all_gather | solution.py:52
  119.4 36.1 %while.51 = (s32[]{:T(128)}, f32[8,4,128]{2,1,0:T(4,128)S(1)}, f32[8,4,128]{2,1,0:T(4,128)S(1)}, s32[8]{0:T(128)S(1)}, s32[64,64]{0,1:T(8,128)}, /*index=5*/s32[...) while((s32[]{:T(128)}, f32[8,4,128]{2,1,0:T(4,128)S(1)}, ...), condition=%wide.region_8.9_spmd, body=%wide.region_2.8_spmd.sunk | while | flops 151265344 | bytes 24269540 | solution.py:97
  122.8 8.4 %conditional.6 = ((f32[8,4,128]{2,1,0:T(4,128)S(1)}, f32[8,4,128]{2,1,0:T(4,128)S(1)})) conditional(s32[]{:T(128)} %convert_element_type.205, (f32[8,4,128]{2,1,0:T(4,128)S(1)}, f32[8,4,128]{2,1,0:T(4,128)S(1)}) %tuple.175, (s32[2,8]{0,1:T(8,128)S(1)}, s32[]{:T(128)}, pred[]{:T(512)}, bf16[8,4096,256]{1,2,0:T(8,128)(2,1)}, ...), branch_computations={%region_4.4_spmd, %region_5.7_spmd} | conditional | flops 151265296 | bytes 24268952 | solution.py:91
  124.2 1.8 constant_dynamic-slice_fusion
  126.0 3.0 fusion.1
  129.0 2.1 select_reduce_fusion
  156.9 37.0 %while.52 = (s32[]{:T(128)}, f32[8,128,4,32]{1,3,2,0:T(8,128)}, s32[8]{0:T(128)S(1)}, s32[64,64]{0,1:T(8,128)}, s32[]{:T(128)}, /*index=5*/bf16[8,4096,256]{1,2,...) while((s32[]{:T(128)}, f32[8,128,4,32]{1,3,2,0:T(8,128)}, ...), condition=%wide.region_13.14_spmd, body=%wide.region_9.13_spmd.sunk | while | flops 277217376 | bytes 10375892 | solution.py:118
  160.2 10.1 %conditional.7 = (f32[8,128,4,32]{1,3,2,0:T(8,128)}) conditional(s32[]{:T(128)} %convert_element_type.206, f32[8,128,4,32]{1,3,2,0:T(8,128)} %get-tuple-element.1564, (s32[2,8]{0,1:T(8,128)S(1)}, s32[]{:T(128)}, pred[]{:T(512)}, bf16[8,4096,256]{1,2,0:T(8,128)(2,1)}, bf16[8,128,4,32]{1,3,2,0:T(8,128)(2,1)}, ...), branch_computations={%region_11.11_spmd, %region_12.12_spmd} | conditional | flops 277217312 | bytes 10375321 | solution.py:114
  160.3 3.3 constant_dynamic-slice_fusion.2
  165.5 4.8 fusion.14
  193.9 2.3 bitcast_reduce_fusion
  197.1 97.8 %while.53 = (s32[]{:T(128)}, f32[8,128,4,32]{1,3,2,0:T(8,128)}, bf16[8,512,4,128]{3,1,0,2:T(8,128)(2,1)}, bf16[8,512,8,128]{3,2,1,0:T(8,128)(2,1)}, s32[8]{0:T(1...) while((s32[]{:T(128)}, f32[8,128,4,32]{1,3,2,0:T(8,128)}, ...), condition=%wide.region_20.21_spmd, body=%wide.region_15.20_spmd.sunk | while | flops 2305949696 | bytes 124179344 | solution.py:182
  200.5 34.9 %conditional.8 = (f32[8,128,4,32]{1,3,2,0:T(8,128)}, bf16[1,512,4,128]{3,1,2,0:T(8,128)(2,1)}, bf16[1,512,8,128]{3,1,2,0:T(8,128)(2,1)S(1)}) conditional(s32[]{:T(128)} %convert_element_type.207, f32[8,128,4,32]{1,3,2,0:T(8,128)} %get-tuple-element.1617, (s32[2,8]{0,1:T(8,128)S(1)}, s32[]{:T(128)}, pred[]{:T(512)}, ...), branch_computations={%region_17.17_spmd, %region_18.19_spmd} | conditional | flops 2305949696 | bytes 121032976 | solution.py:180
  200.5 3.3 constant_dynamic-slice_fusion.4
  205.0 5.5 fusion.75
  210.7 6.9 fusion.73
  217.6 2.9 fusion.39
  220.5 1.8 fusion.26
  222.3 1.8 copy.94
  224.1 3.7 fusion.29
  227.9 1.9 copy.93
  229.7 5.6 fusion.33
  235.4 1.9 bitcast_dynamic-update-slice_fusion.2
  237.3 1.7 copy_dynamic-update-slice_fusion.2
  243.4 1.9 bitcast_dynamic-update-slice_fusion.2
  245.3 1.7 copy_dynamic-update-slice_fusion.2
  251.3 1.9 bitcast_dynamic-update-slice_fusion.2
  259.3 1.9 bitcast_dynamic-update-slice_fusion.2
  261.2 1.7 copy_dynamic-update-slice_fusion.2
  267.3 2.0 bitcast_dynamic-update-slice_fusion.2
  269.3 1.7 copy_dynamic-update-slice_fusion.2
  275.3 1.9 bitcast_dynamic-update-slice_fusion.2
  283.3 1.9 bitcast_dynamic-update-slice_fusion.2
  285.2 1.7 copy_dynamic-update-slice_fusion.2
  291.3 2.0 bitcast_dynamic-update-slice_fusion.2
  293.2 1.7 copy_dynamic-update-slice_fusion.2
  295.5 412.1 %reduce-scatter.5.cloned.1.call-done = bf16[1024,4,128]{2,0,1:T(8,128)(2,1)} async-done(((bf16[4096,4,128]{2,0,1:T(8,128)(2,1)}), bf16[1024,4,128]{2,0,1:T(8,128)(2,1)}) %reduce-scatter.5.cloned.1.call-update) | async-done | bytes 1048592 | tf_op jit(solution)/shard_map/reduce_scatter | solution.py:201
  707.6 3.0 copy.118
  710.6 7.7 all-to-all-start
  724.4 2.0 convolution_convert_fusion.1
  726.4 8.8 %all-to-all-done = bf16[1024,4,128]{2,1,0:T(4,128)(2,1)S(1)} async-done(((bf16[1024,4,128]{2,1,0:T(4,128)(2,1)}), bf16[1024,4,128]{2,1,0:T(4,128)(2,1)S(1)}, u32[]{:S(2)}, u32[]{:S(2)}) %all-to-all-start) | async-done | bytes 1048608 | tf_op jit(solution)/shard_map/all_to_all | solution.py:204
  736.9 1.7 reshape.247
  738.6 64.0 %reduce-scatter.3.cloned.1.call-done = bf16[128,8,128]{2,1,0:T(8,128)(2,1)} async-done(((bf16[4096,8,128]{2,1,0:T(8,128)(2,1)}), bf16[128,8,128]{2,1,0:T(8,128)(2,1)}) %reduce-scatter.3.cloned.1.call-update) | async-done | bytes 262160 | tf_op jit(solution)/shard_map/reduce_scatter | solution.py:187
  (199 shorter events, 95.4 us)
Async XLA Ops:
  7.2 186.8 %copy-start = (bf16[8,128,128]{2,1,0:T(8,128)(2,1)S(1)}, bf16[8,128,128]{2,1,0:T(8,128)(2,1)}, u32[]{:S(2)}) copy-start(bf16[8,128,128]{2,1,0:T(8,128)(2,1)} %param.23) | copy-start | bytes 786436
  7.2 14.0 %slice-start = ((bf16[128,512]{1,0:T(8,128)(2,1)}), bf16[128,256]{1,0:T(8,128)(2,1)S(1)}, s32[]{:S(2)}) async-start(bf16[128,512]{1,0:T(8,128)(2,1)} %param.21), calls=%async_computation.7 | async-start | bytes 131072
  7.2 62.6 %copy-start.10 = (bf16[128,512]{1,0:T(8,128)(2,1)S(1)}, bf16[128,512]{1,0:T(8,128)(2,1)}, u32[]{:S(2)}) copy-start(bf16[128,512]{1,0:T(8,128)(2,1)} %param.21) | copy-start | bytes 393220
  7.2 62.6 %all-gather.3.cloned.1.call-start = ((), (), s32[]{:S(2)}) async-start(), calls=%async_computation.3 | async-start | bytes 8650752 | tf_op jit(solution)/shard_map/all_gather | solution.py:53
  8.4 1.9 copy-start.13
  9.7 0.6 copy-start.18
  10.3 0.6 copy-start.16
  13.0 106.4 %all-gather.5.cloned.1.call-start = ((), (), s32[]{:S(2)}) async-start(), calls=%async_computation.4 | async-start | bytes 5242880 | tf_op jit(solution)/shard_map/all_gather | solution.py:52
  15.3 692.3 %reduce-scatter.5.cloned.1.call-start = ((), (), s32[]{:S(2)}) async-start(), calls=%async_computation.6 | async-start | bytes 5242880 | tf_op jit(solution)/shard_map/reduce_scatter | solution.py:201
  20.2 64.1 %copy-start.7 = (f32[1024,128]{1,0:T(8,128)}, f32[1024,128]{1,0:T(8,128)S(1)}, u32[]{:S(2)}) copy-start(f32[1024,128]{1,0:T(8,128)S(1)} %fusion.47) | copy-start | bytes 1572868
  200.5 10.2 %copy-start.20 = (f32[8,4,128]{2,1,0:T(4,128)S(1)}, f32[8,4,128]{2,1,0:T(4,128)}, u32[]{:S(2)}) copy-start(f32[8,4,128]{2,1,0:T(4,128)} %get-tuple-element.1016) | copy-start | bytes 49156 | tf_op jit(solution)/shard_map/while/body/eval_jaxpr/cond
  210.7 9.9 %copy-start.3 = (f32[8,4,512,128]{3,2,1,0:T(8,128)S(1)}, f32[8,4,512,128]{3,2,1,0:T(8,128)}, u32[]{:S(2)}) copy-start(f32[8,4,512,128]{3,2,1,0:T(8,128)} %fusion.75) | copy-start | bytes 25165828 | tf_op jit(solution)/shard_map/while/body/eval_jaxpr/cond
  210.7 9.8 %copy-start.12 = (bf16[8,128,4,32]{1,3,2,0:T(8,128)(2,1)S(1)}, bf16[8,128,4,32]{1,3,2,0:T(8,128)(2,1)}, u32[]{:S(2)}) copy-start(bf16[8,128,4,32]{1,3,2,0:T(8,128)(2,1)} %get-tuple-element.1017) | copy-start | bytes 786436 | tf_op jit(solution)/shard_map/while/body/eval_jaxpr/cond
  217.6 4.7 copy-start.2
  294.9 423.4 %copy-start.11 = (bf16[128,512]{1,0:T(8,128)(2,1)S(1)}, bf16[128,512]{1,0:T(8,128)(2,1)}, u32[]{:S(2)}) copy-start(bf16[128,512]{1,0:T(8,128)(2,1)} %param.21) | copy-start | bytes 393220
  294.9 425.9 %copy-start.5 = (f32[8,128,128]{1,2,0:T(8,128)S(1)}, f32[8,128,128]{1,2,0:T(8,128)}, u32[]{:S(2)}) copy-start(f32[8,128,128]{1,2,0:T(8,128)} %copy.106) | copy-start | bytes 1572868
  295.0 425.9 %copy-start.6 = (f32[8,128,128]{1,2,0:T(8,128)S(1)}, f32[8,128,128]{1,2,0:T(8,128)}, u32[]{:S(2)}) copy-start(f32[8,128,128]{1,2,0:T(8,128)} %get-tuple-element.1269) | copy-start | bytes 1572868
  295.0 507.7 %reduce-scatter.3.cloned.1.call-start = ((), (), s32[]{:S(2)}) async-start(), calls=%async_computation.5 | async-start | bytes 8650752 | tf_op jit(solution)/shard_map/reduce_scatter | solution.py:187
  295.0 429.4 %copy-start.8 = (f32[1024,128]{1,0:T(8,128)S(1)}, f32[1024,128]{1,0:T(8,128)}, u32[]{:S(2)}) copy-start(f32[1024,128]{1,0:T(8,128)} %copy-done.7) | copy-start | bytes 1572868
  295.0 429.4 %copy-start.15 = (bf16[128,128]{1,0:T(8,128)(2,1)S(1)}, bf16[128,128]{1,0:T(8,128)(2,1)}, u32[]{:S(2)}) copy-start(bf16[128,128]{1,0:T(8,128)(2,1)} %param.22) | copy-start | bytes 98308
  710.6 24.6 %all-to-all-start = ((bf16[1024,4,128]{2,1,0:T(4,128)(2,1)}), bf16[1024,4,128]{2,1,0:T(4,128)(2,1)S(1)}, u32[]{:S(2)}, u32[]{:S(2)}) async-start(bf16[1024,4,128]{2,1,0:T(4,128)(2,1)} %copy.118), calls=%async_computation.2 | async-start | bytes 2097152 | tf_op jit(solution)/shard_map/all_to_all | solution.py:204
  726.4 77.3 %copy-start.9 = (bf16[16,8,8,128]{3,1,2,0:T(8,128)(2,1)S(1)}, bf16[16,8,8,128]{3,1,2,0:T(8,128)(2,1)}, u32[]{:S(2)}) copy-start(bf16[16,8,8,128]{3,1,2,0:T(8,128)(2,1)} %copy.145) | copy-start | bytes 786436
  726.4 77.7 %copy-start.4 = (bf16[8,128,128]{2,1,0:T(8,128)(2,1)S(1)}, bf16[8,128,128]{2,1,0:T(8,128)(2,1)}, u32[]{:S(2)}) copy-start(bf16[8,128,128]{2,1,0:T(8,128)(2,1)} %param.18) | copy-start | bytes 786436
  726.4 77.7 %copy-start.14 = (f32[8,128]{1,0:T(8,128)S(1)}, f32[8,128]{1,0:T(8,128)}, u32[]{:S(2)}) copy-start(f32[8,128]{1,0:T(8,128)} %copy-done.13) | copy-start | bytes 12292
  735.4 69.1 %copy-start.19 = (f32[8,128]{1,0:T(8,128)S(1)}, f32[8,128]{1,0:T(8,128)}, u32[]{:S(2)}) copy-start(f32[8,128]{1,0:T(8,128)} %copy-done.18) | copy-start | bytes 12292
  735.4 69.2 %copy-start.17 = (f32[8,128]{1,0:T(8,128)S(1)}, f32[8,128]{1,0:T(8,128)}, u32[]{:S(2)}) copy-start(f32[8,128]{1,0:T(8,128)} %copy-done.16) | copy-start | bytes 12292
  735.4 71.1 %copy-start.1 = (bf16[8,128,128]{2,1,0:T(8,128)(2,1)S(1)}, bf16[8,128,128]{2,1,0:T(8,128)(2,1)}, u32[]{:S(2)}) copy-start(bf16[8,128,128]{2,1,0:T(8,128)(2,1)} %param.23) | copy-start | bytes 786436
Sparse Core Ops, SparseCore 0:
  13.1 56.6 all-gather.2
  72.1 47.2 all-gather.4
  295.1 412.5 reduce-scatter.4
  711.7 90.9 reduce-scatter.2
where the time goes:
time: 820 us; the launch traced here: 813 us
  waiting for transfers between devices  548 us (67%)
  local copies, waits for them, and re-layouts  103 us (13%)
  matrix products  55.9 us (7%)
  other arithmetic  51.1 us (6%)
  loops' own time  33.2 us (4%)
  between operations  14.2 us (2%)
    reduce_scatter x1, waiting for transfers between devices, on_device(): lax.psum_scatter(bias_terms.astype(jnp.bfloat16), 'row', scatter_dimensio...  412 us
    reduce_scatter x1, waiting for transfers between devices, on_device(): lax.psum_scatter(pair_terms.astype(jnp.bfloat16), 'col', scatter_dimensio...  64 us
    all_gather x1, waiting for transfers between devices, on_device(): gathered_slab = lax.all_gather(normed, 'col', axis=1, tiled=True)  48.5 us
    dynamic_update_slice x16, local copies, waits for them, and re-layouts, on_device(): lax.scan(grad_step, jnp.zeros((row_count, col_count, H, DH), jnp.float32)...  28.8 us
    while x4, local copies, waits for them, and re-layouts, on_device(): lax.scan(value_step, jnp.zeros((row_count, col_count, H, DH), jnp.float32...  24.7 us
  transfers between devices with their start and end apart: 5, of which 5 were waited for; matrix products, arithmetic and copies ran while one was open for 7% of the time, Pallas kernels for 0%

commit v1 on v0

v1 whole, which is shorter than its diff:
```python
import functools

import jax
import jax.numpy as jnp
from jax import lax
from jax.experimental import pallas as pl
from jax.experimental.pallas import tpu as pltpu
from jax.sharding import PartitionSpec as P

H = 4
DH = 32
TILE = 64
HJ = H * TILE

eps_norm = 1e-05
neg_big = -1e30
CT = 4
F32 = jnp.float32
BF16 = jnp.bfloat16


def nt(a, b):
    return lax.dot_general(a, b, (((1,), (1,)), ((), ())), preferred_element_type=F32)


def tn(a, b):
    return lax.dot_general(a, b, (((0,), (0,)), ((), ())), preferred_element_type=F32)


def nn(a, b):
    return jnp.dot(a, b, preferred_element_type=F32)


def head_blocks(rows, chans):
    row_head = lax.broadcasted_iota(jnp.int32, (rows, chans), 0) // TILE
    col_head = lax.broadcasted_iota(jnp.int32, (rows, chans), 1) // DH
    return row_head == col_head


def diagonal(full_t):
    parts = [full_t[h * DH : (h + 1) * DH, h * TILE : (h + 1) * TILE] for h in range(H)]
    return jnp.transpose(jnp.concatenate(parts, axis=0))


def attention_kernel(
    place_ref, mask_ref, x_ref, bias_ref, d_out_ref, w_proj_ref, w_out_ref,
    out_ref, dn_ref, pair_ref, bias_grad_ref,
    k_ref, v_ref, q_ref, do_ref, bias_f, grad_f, max_ref, sum_ref, delta_ref, acc_ref,
    gate_ref, dg_ref, list_ref,
):
    c = place_ref[0]
    tiles = 2 * x_ref.shape[0]
    rows = x_ref.shape[1]
    width = H * DH
    q_scale = DH ** (-0.5)
    query_tiles = (2 * c, tiles - 1 - 2 * c)
    w_q = w_proj_ref[:, :width]
    w_pair = w_proj_ref[:, width : 3 * width]
    w_gate = w_proj_ref[:, 3 * width :]

    def project(block, _):
        for r in range(rows):
            kv = nn(x_ref[block, r], w_pair).astype(BF16)
            for half in range(2):
                k_ref[2 * block + half, r] = kv[half * TILE : (half + 1) * TILE, :width]
                v_ref[2 * block + half, r] = kv[half * TILE : (half + 1) * TILE, width:]
        return 0

    lax.fori_loop(0, jnp.maximum(c, tiles // 2 - 1 - c) + 1, project, 0)

    counts, idles = [], []
    for a in range(2):
        def scan_tile(b, carried, a=a):
            count, idle = carried
            live = mask_ref[query_tiles[a], b] > 0
            list_ref[a, count] = b
            return jnp.where(live, count + 1, count), jnp.where(live, idle, b)

        count, idle = lax.fori_loop(0, tiles, scan_tile, (jnp.int32(0), jnp.int32(0)))
        for extra in range(CT):
            list_ref[a, count + extra] = query_tiles[a]
        counts.append(count)
        idles.append(idle)

    blocks = head_blocks(HJ, width)
    for a in range(2):
        tile = query_tiles[a]

        def prepare(r, _, a=a, tile=tile):
            x_q = x_ref[tile // 2, r, pl.ds(pl.multiple_of((tile % 2) * TILE, TILE), TILE), :]
            queries = (nn(x_q, w_q) * q_scale).astype(BF16)
            gating = jax.nn.sigmoid(nn(x_q, w_gate))
            d_gated = nt(d_out_ref[a, r], w_out_ref[...])
            d_att = (d_gated * gating).astype(BF16)
            zero = jnp.zeros((HJ, width), BF16)
            q_ref[a, r] = jnp.where(blocks, jnp.concatenate([queries] * H, axis=0), zero)
            do_ref[a, r] = jnp.where(blocks, jnp.concatenate([d_att] * H, axis=0), zero)
            gate_ref[a, r] = gating
            dg_ref[a, r] = d_gated
            return 0

        lax.fori_loop(0, rows, prepare, 0)

    def load_chunk(a, n):
        ids = [list_ref[a, n * CT + t] for t in range(CT)]
        for t in range(CT):
            block = bias_ref[a, ids[t]].astype(F32)
            shut = jnp.where(n * CT + t < counts[a], 0.0, neg_big)
            bias_f[t * TILE : (t + 1) * TILE, :] = block + shut
        return ids

    max_ref[...] = jnp.full(max_ref.shape, neg_big, F32)
    sum_ref[...] = jnp.zeros(sum_ref.shape, F32)
    acc_ref[...] = jnp.zeros(acc_ref.shape, F32)
    for a in range(2):
        def forward(n, _, a=a):
            ids = load_chunk(a, n)

            def per_row(r):
                keys = jnp.concatenate([k_ref[i, r] for i in ids], axis=0)
                values = jnp.concatenate([v_ref[i, r] for i in ids], axis=0)
                scores = nt(keys, q_ref[a, r]) + bias_f[...]
                old = max_ref[a, r]
                new = jnp.maximum(old, jnp.max(scores, axis=0, keepdims=True))
                fade = jnp.exp(old - new)
                probs = jnp.exp(scores - new)
                max_ref[a, r] = new
                sum_ref[a, r] = sum_ref[a, r] * fade + jnp.sum(probs, axis=0, keepdims=True)
                acc_ref[a, r] = acc_ref[a, r] * fade + tn(values, probs.astype(BF16))

            def some_rows(step, _):
                for u in range(2):
                    per_row(step * 2 + u)
                return 0

            lax.fori_loop(0, rows // 2, some_rows, 0)
            return 0

        lax.fori_loop(0, (counts[a] + CT - 1) // CT, forward, 0)

    for a in range(2):
        def middle(r, _, a=a):
            total = sum_ref[a, r]
            full_t = acc_ref[a, r] * (1.0 / total)
            max_ref[a, r] = max_ref[a, r] + jnp.log(total)
            delta_ref[a, r] = jnp.sum(
                full_t * jnp.transpose(do_ref[a, r].astype(F32)), axis=0, keepdims=True
            )
            attended = diagonal(full_t)
            gating = gate_ref[a, r]
            gated = (gating * attended).astype(BF16)
            out_ref[a, r] = nn(gated, w_out_ref[...]).astype(BF16)
            dg_ref[a, r] = dg_ref[a, r] * attended * gating * (1.0 - gating)
            acc_ref[a, r] = jnp.zeros(acc_ref.shape[2:], F32)
            return 0

        lax.fori_loop(0, rows, middle, 0)

    def clear(b, _):
        pair_ref[b] = jnp.zeros(pair_ref.shape[1:], BF16)
        for a in range(2):
            bias_grad_ref[a, b] = jnp.zeros(bias_grad_ref.shape[2:], BF16)
        return 0

    lax.fori_loop(0, tiles, clear, 0)
    for a in range(2):
        def backward(n, _, a=a):
            ids = load_chunk(a, n)

            def per_row(r, first):
                keys = jnp.concatenate([k_ref[i, r] for i in ids], axis=0)
                values = jnp.concatenate([v_ref[i, r] for i in ids], axis=0)
                q = q_ref[a, r]
                do = do_ref[a, r]
                probs = jnp.exp(nt(keys, q) + bias_f[...] - max_ref[a, r])
                d_scores = probs * (nt(values, do) - delta_ref[a, r])
                if first is None:
                    grad_f[...] += d_scores
                else:
                    grad_f[...] = jnp.where(first, d_scores, grad_f[...] + d_scores)
                d_b = d_scores.astype(BF16)
                acc_ref[a, r] += tn(keys, d_b)
                d_keys = nn(d_b, q)
                d_values = nn(probs.astype(BF16), do)
                both = jnp.concatenate([d_keys, d_values], axis=1).astype(BF16)
                term = nt(both, w_pair)
                for t in range(CT):
                    piece = term[t * TILE : (t + 1) * TILE]
                    pair_ref[ids[t], r] = (pair_ref[ids[t], r].astype(F32) + piece).astype(BF16)

            def some_rows(step, _):
                for u in range(2):
                    per_row(step * 2 + u, (step == 0) if u == 0 else None)
                return 0

            lax.fori_loop(0, rows // 2, some_rows, 0)
            for t in range(CT):
                target = jnp.where(n * CT + t < counts[a], ids[t], idles[a])
                bias_grad_ref[a, target] = grad_f[t * TILE : (t + 1) * TILE, :].astype(BF16)
            return 0

        lax.fori_loop(0, (counts[a] + CT - 1) // CT, backward, 0)

    for a in range(2):
        def finish(r, _, a=a):
            d_q = diagonal(acc_ref[a, r]) * q_scale
            d_q = nt(d_q.astype(BF16), w_q)
            dn_ref[a, r] = (d_q + nt(dg_ref[a, r].astype(BF16), w_gate)).astype(BF16)
            return 0

        lax.fori_loop(0, rows, finish, 0)


def attention(place, mask, x_all, bias_t, d_out, w_proj, w_out):
    blocks, rows, cols, chans = x_all.shape
    tiles = blocks * cols // TILE
    width = H * DH
    vmem = pl.BlockSpec(memory_space=pltpu.VMEM)
    smem = pl.BlockSpec(memory_space=pltpu.SMEM)
    return pl.pallas_call(
        attention_kernel,
        out_shape=(
            jax.ShapeDtypeStruct((2, rows, TILE, chans), BF16),
            jax.ShapeDtypeStruct((2, rows, TILE, chans), BF16),
            jax.ShapeDtypeStruct((tiles, rows, TILE, chans), BF16),
            jax.ShapeDtypeStruct((2, tiles, TILE, HJ), BF16),
        ),
        in_specs=[smem, smem, vmem, vmem, vmem, vmem, vmem],
        out_specs=(vmem,) * 4,
        scratch_shapes=[
            pltpu.VMEM((tiles, rows, TILE, width), BF16),
            pltpu.VMEM((tiles, rows, TILE, width), BF16),
            pltpu.VMEM((2, rows, HJ, width), BF16),
            pltpu.VMEM((2, rows, HJ, width), BF16),
            pltpu.VMEM((CT * TILE, HJ), F32),
            pltpu.VMEM((CT * TILE, HJ), F32),
            pltpu.VMEM((2, rows, 1, HJ), F32),
            pltpu.VMEM((2, rows, 1, HJ), F32),
            pltpu.VMEM((2, rows, 1, HJ), F32),
            pltpu.VMEM((2, rows, width, HJ), F32),
            pltpu.VMEM((2, rows, TILE, width), F32),
            pltpu.VMEM((2, rows, TILE, width), F32),
            pltpu.SMEM((2, tiles + CT), jnp.int32),
        ],
        compiler_params=pltpu.CompilerParams(vmem_limit_bytes=60 * 1024 * 1024),
        name="attention",
    )(place, mask, x_all, bias_t, d_out, w_proj, w_out)


def on_device(pair_slab, pair_bias, tile_mask, w_proj, w_out, d_out):
    rows, cols, chans = pair_slab.shape
    ncol = lax.axis_size("col")
    flip = [(i, ncol - 1 - i) for i in range(ncol)]
    c = lax.axis_index("col")
    entries = pair_slab.astype(F32)
    centred = entries - jnp.mean(entries, axis=-1, keepdims=True)
    spread = jnp.mean(centred * centred, axis=-1, keepdims=True)
    rstd = lax.rsqrt(spread + eps_norm)
    normed_f = centred * rstd
    x_all = lax.all_gather(normed_f.astype(BF16), "col", axis=0)

    halves = pair_bias.reshape(H, 2, TILE, -1).transpose(1, 3, 0, 2).reshape(2, -1, HJ)
    bias_pair = jnp.stack([halves[0], lax.ppermute(halves[1], "col", flip)])
    bias_t = lax.all_gather(bias_pair, "row", axis=1, tiled=True)
    bias_t = bias_t.reshape(2, -1, TILE, HJ)
    d_out_h = d_out.reshape(rows, 2, TILE, chans).transpose(1, 0, 2, 3)
    d_out_pair = jnp.stack([d_out_h[0], lax.ppermute(d_out_h[1], "col", flip)])

    out, dn, pair, bias_grad = attention(
        c.reshape(1).astype(jnp.int32), tile_mask, x_all, bias_t, d_out_pair, w_proj, w_out
    )

    out_odd = lax.ppermute(out[1], "col", flip)
    attn_out = jnp.stack([out[0], out_odd], axis=1).reshape(rows, cols, chans)
    dn_odd = lax.ppermute(dn[1], "col", flip)
    dn_own = jnp.stack([dn[0], dn_odd], axis=1).reshape(rows, cols, chans).astype(F32)
    pair_sum = lax.psum_scatter(pair, "col", scatter_dimension=0, tiled=True)
    pair_sum = pair_sum.transpose(1, 0, 2, 3).reshape(rows, cols, chans)
    d_normed = dn_own + pair_sum.astype(F32)
    slab_grads = rstd * (
        d_normed
        - jnp.mean(d_normed, axis=-1, keepdims=True)
        - normed_f * jnp.mean(d_normed * normed_f, axis=-1, keepdims=True)
    )
    grads = bias_grad.reshape(2, -1, HJ)
    grads = lax.psum_scatter(grads, "row", scatter_dimension=1, tiled=True)
    grads = grads.reshape(2, ncol, -1, H, TILE)
    grads = lax.all_to_all(grads, "col", split_axis=1, concat_axis=1, tiled=True)
    even = grads[0]
    odd = grads[1][::-1]
    both = jnp.stack([even, odd], axis=1).astype(F32)
    bias_grads = both.transpose(2, 3, 0, 1, 4).reshape(-1, H, ncol * cols)
    return attn_out, slab_grads.astype(BF16), bias_grads


def solution(mesh):
    in_specs = (P("row", "col", None), P(None, "col", "row"), P(), P(), P(), P("row", "col", None))
    out_specs = (P("row", "col", None), P("row", "col", None), P(("row", "col"), None, None))
    return jax.shard_map(
        on_device, mesh=mesh, in_specs=in_specs, out_specs=out_specs, check_vma=False
    )
```

time: 820 us -> 403 us (0.49)
  waiting for transfers between devices: 548 us -> 232 us
  Pallas kernels: 0 us -> 88.2 us
  local copies, waits for them, and re-layouts: 103 us -> 34.1 us
  matrix products: 55.9 us -> 0 us
  other arithmetic: 51.1 us -> 6.94 us
  loops' own time: 33.2 us -> 0 us
  starting transfers between devices: 7.81 us -> 26.5 us
    reduce_scatter x2, waiting for transfers between devices: 476 us -> 113 us  [the longest x1 72.7 us: on_device(): grads = lax.psum_scatter(grads, 'row', scatter_dimension=1, tiled=True)]
    pallas_call x0 -> x1, Pallas kernels: none -> 88.2 us  [attention(): pl.pallas_call(attention_kernel, out_shape=(jax.ShapeDtypeStruct((2, rows...]
    dot_general x14 -> x0, matrix products: 55.9 us -> none  [the longest x1 14.5 us: on_device(): jnp.dot(gathered_slab.reshape(-1, channels), w_pair, preferred_element_ty...]
    reduce_or x24 -> x0, other arithmetic: 34.5 us -> none  [the longest x8 11.9 us: stats_step(): jnp.any(tile_block > 0)]
    another operation x27 -> x0, loops' own time: 33.2 us -> none  [the longest x1 11.1 us: on_device(): lax.scan(stats_step, (start_max, start_sum), block_ids)]
    ppermute x0 -> x4, waiting for transfers between devices: none -> 30 us  [the longest x1 14.8 us: on_device(): out_odd = lax.ppermute(out[1], 'col', flip)]
    dynamic_update_slice x16 -> x0, local copies, waits for them, and re-layouts: 28.8 us -> none  [on_device(): lax.scan(grad_step, jnp.zeros((row_count, col_count, H, DH), jnp.float32)...]
    all_gather x2, waiting for transfers between devices: 62.3 us -> 88 us  [the longest x1 50.3 us: on_device(): x_all = lax.all_gather(normed_f.astype(BF16), 'col', axis=0)]
  transfers between devices with their start and end apart: 5 -> 9, of which waited for: 5 -> 7; matrix products, arithmetic and copies ran while one was open for 7% -> 9% of each run, Pallas kernels for 0% -> 0%
where the time goes in v1:
time: 403 us; the launch traced here: 402 us
  waiting for transfers between devices  232 us (58%)
  Pallas kernels  88.2 us (22%)
  local copies, waits for them, and re-layouts  34.1 us (8%)
  starting transfers between devices  26.5 us (7%)
  between operations  14 us (3%)
  other arithmetic  6.94 us (2%)
    pallas_call x1, Pallas kernels, attention(): pl.pallas_call(attention_kernel, out_shape=(jax.ShapeDtypeStruct((2, rows...  88.2 us
    reduce_scatter x1, waiting for transfers between devices, on_device(): grads = lax.psum_scatter(grads, 'row', scatter_dimension=1, tiled=True)  72.7 us
    all_gather x1, waiting for transfers between devices, on_device(): x_all = lax.all_gather(normed_f.astype(BF16), 'col', axis=0)  50.3 us
    reduce_scatter x1, waiting for transfers between devices, on_device(): pair_sum = lax.psum_scatter(pair, 'col', scatter_dimension=0, tiled=True)  40.5 us
    all_gather x1, waiting for transfers between devices, on_device(): bias_t = lax.all_gather(bias_pair, 'row', axis=1, tiled=True)  37.7 us
    unnamed x14, local copies, waits for them, and re-layouts  18.2 us
    ppermute x1, waiting for transfers between devices, on_device(): out_odd = lax.ppermute(out[1], 'col', flip)  14.8 us
    ppermute x1, waiting for transfers between devices, on_device(): bias_pair = jnp.stack([halves[0], lax.ppermute(halves[1], 'col', flip)])  11.7 us
  transfers between devices with their start and end apart: 9, of which 7 were waited for; matrix products, arithmetic and copies ran while one was open for 9% of the time, Pallas kernels for 0%

profile of v1, /device:TPU:1, one launch (start us, length us, event | category | flops | bytes accessed | tf_op | source)
XLA Modules:
  0.0 401.5 jit_solution(6327312418991215423)
XLA Ops:
  7.2 0.0 all-gather.4.cloned.1.call-start
  7.2 1.4 fusion.12
  8.6 7.7 %collective-permute-start = (bf16[1024,256]{0,1:T(8,128)(2,1)S(1)}, bf16[1024,256]{0,1:T(8,128)(2,1)S(1)}, u32[]{:S(2)}, u32[]{:S(2)}) collective-permute-start(bf16[1024,256]{0,1:T(8,128)(2,1)S(1)} %bitcast.62), channel_id=1, source_target_pairs={{0,31},{1,30},{2,29},{3,28},{4,27},{5,26},{6,25},{7,24},{8,23},{9,... | collective-permute-start | bytes 1572872 | tf_op jit(solution)/shard_map/ppermute | solution.py:263
  16.3 11.7 %collective-permute-done = bf16[1024,256]{0,1:T(8,128)(2,1)S(1)} collective-permute-done((bf16[1024,256]{0,1:T(8,128)(2,1)S(1)}, bf16[1024,256]{0,1:T(8,128)(2,1)S(1)}, u32[]{:S(2)}, u32[]{:S(2)}) %collective-permute-start) | collective-permute-done | bytes 524320 | tf_op jit(solution)/shard_map/ppermute | solution.py:263
  28.0 1.1 pad_maximum_fusion
  29.1 0.0 all-gather.4.cloned.1.call-update
  29.1 0.0 all-gather.6.cloned.1.call-start
  29.1 0.1 convert_reduce_fusion
  29.3 0.4 fusion.9
  29.7 1.1 fusion.4
  30.7 0.0 all-gather.6.cloned.1.call-update
  30.8 0.0 reduce-scatter.5.cloned.1.call-start
  30.9 5.9 %collective-permute-start.1 = (bf16[8,64,128]{2,1,0:T(8,128)(2,1)S(1)}, bf16[8,64,128]{2,1,0:T(8,128)(2,1)S(1)}, u32[]{:S(2)}, u32[]{:S(2)}) collective-permute-start(bf16[8,64,128]{2,1,0:T(8,128)(2,1)S(1)} %get-tuple-element.31), channel_id=1, source_target_pairs={{0,31},{1,30},{2,29},{3,28},{4,27},{5,26},{6,25},{7,24},{8,23},{9,... | collective-permute-start | bytes 393224 | tf_op jit(solution)/shard_map/ppermute | solution.py:267
  36.8 3.5 collective-permute-done.1
  40.2 0.7 pad_maximum_fusion.1.d_out_ref
  41.0 37.7 %all-gather.4.cloned.1.call-done = bf16[2,4096,256]{1,2,0:T(8,128)(2,1)} async-done(((bf16[2,1024,256]{1,2,0:T(8,128)(2,1)}), bf16[2,4096,256]{1,2,0:T(8,128)(2,1)}) %all-gather.4.cloned.1.call-update) | async-done | bytes 4194320 | tf_op jit(solution)/shard_map/all_gather | solution.py:264
  78.7 6.4 %copy.34 = bf16[2,4096,256]{2,1,0:T(8,128)(2,1)} copy(bf16[2,4096,256]{1,2,0:T(8,128)(2,1)} %all-gather.4.cloned.1.call-done) | data formatting | bytes 8388608 | tf_op jit(solution)/shard_map/all_gather | solution.py:264
  85.0 50.3 %all-gather.6.cloned.1.call-done = bf16[256,128,128]{2,1,0:T(8,128)(2,1)} async-done(((bf16[8,128,128]{2,1,0:T(8,128)(2,1)}), bf16[256,128,128]{2,1,0:T(8,128)(2,1)}) %all-gather.6.cloned.1.call-update) | async-done | bytes 8388624 | tf_op jit(solution)/shard_map/all_gather | solution.py:260
  135.4 88.2 %attention.1 = (bf16[2,8,64,128]{3,2,1,0:T(8,128)(2,1)}, bf16[2,8,64,128]{3,2,1,0:T(8,128)(2,1)}, bf16[64,8,64,128]{3,2,1,0:T(8,128)(2,1)}, bf16[2,64,64,256]{3,2,1,0:T(8,128)(2,1)}) custom-call(s32[1]{0:T(128)} %bitcast.place_ref, s32[64,64]{1,0:T(8,128)} %mask_ref.1, bf16[32,8,128,128]{3,2,1,0:T(8,128)(2,1)} %bitcast.52, ...), custom_call_target="tpu_custom_call" | custom-call | tf_op jit(solution)/shard_map/attention/pallas_call | solution.py:220
  223.6 0.0 reduce-scatter.5.cloned.1.call-update
  223.6 0.0 reduce-scatter.3.cloned.1.call-start
  223.6 0.5 reduce-scatter.3.cloned.1.call-update
  224.2 72.7 %reduce-scatter.5.cloned.1.call-done = bf16[2,1024,256]{2,1,0:T(8,128)(2,1)} async-done(((bf16[2,4096,256]{2,1,0:T(8,128)(2,1)}), bf16[2,1024,256]{2,1,0:T(8,128)(2,1)}) %reduce-scatter.5.cloned.1.call-update) | async-done | bytes 1048592 | tf_op jit(solution)/shard_map/reduce_scatter | solution.py:286
  296.9 3.3 reshape.76
  300.2 0.0 copy-start.3
  300.2 2.2 copy.55
  302.4 5.1 %reshape.85 = bf16[32,2,8192]{2,1,0:T(2,128)(2,1)} reshape(bf16[32,2,32,4,64]{4,3,2,1,0:T(4,128)(2,1)} %bitcast.54) | data formatting | bytes 2097152
  307.5 7.6 %all-to-all-start = ((bf16[32,2,8192]{2,1,0:T(2,128)(2,1)}), bf16[32,2,8192]{2,1,0:T(2,128)(2,1)S(1)}, u32[]{:S(2)}, u32[]{:S(2)}) async-start(bf16[32,2,8192]{2,1,0:T(2,128)(2,1)} %reshape.85), calls=%async_computation.2 | async-start | bytes 2097152 | tf_op jit(solution)/shard_map/all_to_all | solution.py:288
  315.2 5.1 %collective-permute-start.2 = (bf16[8,64,128]{2,1,0:T(8,128)(2,1)S(1)}, bf16[8,64,128]{2,1,0:T(8,128)(2,1)S(1)}, u32[]{:S(2)}, u32[]{:S(2)}) collective-permute-start(bf16[8,64,128]{2,1,0:T(8,128)(2,1)S(1)} %get-tuple-element.29), channel_id=1, source_target_pairs={{0,31},{1,30},{2,29},{3,28},{4,27},{5,26},{6,25},{7,24},{8,23},{9,... | collective-permute-start | bytes 393224 | tf_op jit(solution)/shard_map/ppermute | solution.py:273
  320.3 0.7 slice_bitcast_fusion.2
  321.0 0.0 collective-permute-start.3
  321.1 14.8 %collective-permute-done.2 = bf16[8,64,128]{2,1,0:T(8,128)(2,1)S(1)} collective-permute-done((bf16[8,64,128]{2,1,0:T(8,128)(2,1)S(1)}, bf16[8,64,128]{2,1,0:T(8,128)(2,1)S(1)}, u32[]{:S(2)}, u32[]{:S(2)}) %collective-permute-start.2) | collective-permute-done | bytes 131104 | tf_op jit(solution)/shard_map/ppermute | solution.py:273
  335.8 0.7 copy.36
  336.6 0.0 all-to-all-done
  336.6 1.3 reshape.86
  337.9 0.9 fusion.11
  338.8 0.2 copy.53
  339.0 0.2 copy.52
  339.2 0.1 reverse_bitcast_fusion
  339.4 0.5 convert_bitcast_fusion
  339.9 5.2 %copy.44 = f32[32,4,32,2,64]{4,3,2,1,0:T(2,128)} copy(f32[32,4,32,2,64]{4,0,1,3,2:T(8,128)S(1)} %convert_bitcast_fusion) | data formatting | bytes 4194304
  345.1 6.2 %reshape.83 = f32[32,4,4096]{2,1,0:T(4,128)} reshape(f32[32,4,32,2,64]{4,3,2,1,0:T(2,128)} %copy.44) | data formatting | bytes 4194304
  351.3 0.0 collective-permute-done.3
  351.3 40.5 %reduce-scatter.3.cloned.1.call-done = bf16[2,8,64,128]{3,2,1,0:T(8,128)(2,1)} async-done(((bf16[64,8,64,128]{3,2,1,0:T(8,128)(2,1)}), bf16[2,8,64,128]{3,2,1,0:T(8,128)(2,1)}) %reduce-scatter.3.cloned.1.call-update) | async-done | bytes 262160 | tf_op jit(solution)/shard_map/reduce_scatter | solution.py:277
  391.8 1.2 fusion.10
  393.0 0.1 div.17
  393.2 0.5 fusion.5
  393.7 1.3 fusion.8
  (17 shorter events, 0.2 us)
Async XLA Ops:
  7.2 22.0 %copy-start = (bf16[8,128,128]{2,1,0:T(8,128)(2,1)S(1)}, bf16[8,128,128]{2,1,0:T(8,128)(2,1)}, u32[]{:S(2)}) copy-start(bf16[8,128,128]{2,1,0:T(8,128)(2,1)} %param.6) | copy-start | bytes 786436
  7.2 23.6 %copy-start.1 = (bf16[8,128,128]{2,1,0:T(8,128)(2,1)S(1)}, bf16[8,128,128]{2,1,0:T(8,128)(2,1)}, u32[]{:S(2)}) copy-start(bf16[8,128,128]{2,1,0:T(8,128)(2,1)} %param.11) | copy-start | bytes 786436
  7.2 71.5 %all-gather.4.cloned.1.call-start = ((), (), s32[]{:S(2)}) async-start(), calls=%async_computation.3 | async-start | bytes 5242880 | tf_op jit(solution)/shard_map/all_gather | solution.py:264
  8.6 19.4 %collective-permute-start = (bf16[1024,256]{0,1:T(8,128)(2,1)S(1)}, bf16[1024,256]{0,1:T(8,128)(2,1)S(1)}, u32[]{:S(2)}, u32[]{:S(2)}) collective-permute-start(bf16[1024,256]{0,1:T(8,128)(2,1)S(1)} %bitcast.62), channel_id=1, source_target_pairs={{0,31},{1,30},{2,29},{3,28},{4,27},{5,26},{6,25},{7,24},{8,23},{9,... | collective-permute-start | bytes 1572872 | tf_op jit(solution)/shard_map/ppermute | solution.py:263
  29.1 106.3 %all-gather.6.cloned.1.call-start = ((), (), s32[]{:S(2)}) async-start(), calls=%async_computation.6 | async-start | bytes 8650752 | tf_op jit(solution)/shard_map/all_gather | solution.py:260
  30.8 266.1 %reduce-scatter.5.cloned.1.call-start = ((), (), s32[]{:S(2)}) async-start(), calls=%async_computation.5 | async-start | bytes 5242880 | tf_op jit(solution)/shard_map/reduce_scatter | solution.py:286
  30.9 9.4 %collective-permute-start.1 = (bf16[8,64,128]{2,1,0:T(8,128)(2,1)S(1)}, bf16[8,64,128]{2,1,0:T(8,128)(2,1)S(1)}, u32[]{:S(2)}, u32[]{:S(2)}) collective-permute-start(bf16[8,64,128]{2,1,0:T(8,128)(2,1)S(1)} %get-tuple-element.31), channel_id=1, source_target_pairs={{0,31},{1,30},{2,29},{3,28},{4,27},{5,26},{6,25},{7,24},{8,23},{9,... | collective-permute-start | bytes 393224 | tf_op jit(solution)/shard_map/ppermute | solution.py:267
  223.6 168.2 %reduce-scatter.3.cloned.1.call-start = ((), (), s32[]{:S(2)}) async-start(), calls=%async_computation.4 | async-start | bytes 8650752 | tf_op jit(solution)/shard_map/reduce_scatter | solution.py:277
  300.2 15.0 %copy-start.3 = (bf16[2,8,64,128]{3,2,1,0:T(8,128)(2,1)S(1)}, bf16[2,8,64,128]{3,2,1,0:T(8,128)(2,1)}, u32[]{:S(2)}) copy-start(bf16[2,8,64,128]{3,2,1,0:T(8,128)(2,1)} %get-tuple-element.7) | copy-start | bytes 786436
  300.2 20.2 %copy-start.2 = (bf16[2,8,64,128]{3,2,1,0:T(8,128)(2,1)S(1)}, bf16[2,8,64,128]{3,2,1,0:T(8,128)(2,1)}, u32[]{:S(2)}) copy-start(bf16[2,8,64,128]{3,2,1,0:T(8,128)(2,1)} %get-tuple-element.8) | copy-start | bytes 786436
  307.5 29.0 %all-to-all-start = ((bf16[32,2,8192]{2,1,0:T(2,128)(2,1)}), bf16[32,2,8192]{2,1,0:T(2,128)(2,1)S(1)}, u32[]{:S(2)}, u32[]{:S(2)}) async-start(bf16[32,2,8192]{2,1,0:T(2,128)(2,1)} %reshape.85), calls=%async_computation.2 | async-start | bytes 2097152 | tf_op jit(solution)/shard_map/all_to_all | solution.py:288
  315.2 20.6 %collective-permute-start.2 = (bf16[8,64,128]{2,1,0:T(8,128)(2,1)S(1)}, bf16[8,64,128]{2,1,0:T(8,128)(2,1)S(1)}, u32[]{:S(2)}, u32[]{:S(2)}) collective-permute-start(bf16[8,64,128]{2,1,0:T(8,128)(2,1)S(1)} %get-tuple-element.29), channel_id=1, source_target_pairs={{0,31},{1,30},{2,29},{3,28},{4,27},{5,26},{6,25},{7,24},{8,23},{9,... | collective-permute-start | bytes 393224 | tf_op jit(solution)/shard_map/ppermute | solution.py:273
  321.0 30.3 %collective-permute-start.3 = (bf16[8,64,128]{2,1,0:T(8,128)(2,1)}, bf16[8,64,128]{2,1,0:T(8,128)(2,1)}, u32[]{:S(2)}, u32[]{:S(2)}) collective-permute-start(bf16[8,64,128]{2,1,0:T(8,128)(2,1)} %get-tuple-element.27), channel_id=1, source_target_pairs={{0,31},{1,30},{2,29},{3,28},{4,27},{5,26},{6,25},{7,24},{8,23},{9,... | collective-permute-start | bytes 393224 | tf_op jit(solution)/shard_map/ppermute | solution.py:275
Sparse Core Ops, SparseCore 0:
  29.2 49.4 all-gather.3
  81.5 53.8 all-gather.5
  223.7 73.0 reduce-scatter.4
  300.9 90.8 reduce-scatter.2

commit v2 on v1

--- a/solution.py
+++ b/solution.py
@@ -247,34 +247,469 @@
     )(place, mask, x_all, bias_t, d_out, w_proj, w_out)
 
 
+MESH = pl.DeviceIdType.MESH
+RING = 4
+
+
+class Links:
+    def __init__(self, send_sem, recv_sem):
+        self.send_sem, self.recv_sem = send_sem, recv_sem
+        self.count = 0
+        self.sent = []
+
+    def send(self, src, dst, device):
+        n = self.count
+        self.count += 1
+        copy = pltpu.make_async_remote_copy(
+            src_ref=src, dst_ref=dst, send_sem=self.send_sem.at[n], recv_sem=self.recv_sem.at[n],
+            device_id=device, device_id_type=MESH,
+        )
+        copy.start()
+        self.sent.append(copy)
+        return n
+
+    def arrived(self, n, dst):
+        pltpu.make_async_remote_copy(
+            src_ref=dst, dst_ref=dst, send_sem=self.send_sem.at[n], recv_sem=self.recv_sem.at[n],
+            device_id=self.me, device_id_type=MESH,
+        ).wait_recv()
+
+    def finish(self):
+        for copy in self.sent:
+            copy.wait_send()
+
+
+class Place:
+    def __init__(self):
+        self.row = lax.axis_index("row")
+        self.col = lax.axis_index("col")
+        self.core = self.col % 2
+        z = (self.col // 2) % RING
+        y = self.col // (2 * RING)
+        self.yz = (y, z)
+
+    def col_at(self, steps, core=None):
+        y = (self.yz[0] + steps[0]) % RING
+        z = (self.yz[1] + steps[1]) % RING
+        return y * 2 * RING + z * 2 + (self.core if core is None else core)
+
+    def along(self, axis, step):
+        steps = [0, 0]
+        steps[axis] = step
+        return (self.row, self.col_at(steps))
+
+    def along_x(self, step):
+        return ((self.row + step) % RING, self.col)
+
+    def sibling(self):
+        return (self.row, self.col_at((0, 0), 1 - self.core))
+
+    def partner(self):
+        return (self.row, 8 * RING - 1 - self.col)
+
+
+def greet(place):
+    barrier = pltpu.get_barrier_semaphore()
+    others = [place.along(axis, step) for axis in range(2) for step in (1, -1)]
+    others += [place.along_x(1), place.along_x(-1), place.sibling(), place.partner()]
+    for other in others:
+        pl.semaphore_signal(barrier, inc=1, device_id=other, device_id_type=MESH)
+    pl.semaphore_wait(barrier, len(others))
+
+
+def pair_steps(axis, first, second):
+    return (first, second) if axis == 0 else (second, first)
+
+
+def gather_kernel(x_ref, bias_ref, d_ref, x_all, bias_all, d_odd, local_sem, send_sem, recv_sem):
+    place = Place()
+    links = Links(send_sem, recv_sem)
+    links.me = place.sibling()
+    greet(place)
+    rows = x_ref.shape[0]
+    half = rows // 2
+    sub = half // 2
+    long = bias_ref.shape[1]
+    row = place.row
+
+    def spot(steps, start, size, core=None):
+        return x_all.at[place.col_at(steps, core), pl.ds(start, size)]
+
+    def own(start, size):
+        return x_ref.at[pl.ds(start, size)]
+
+    def bias_spot(a, step, start=0, size=None):
+        return bias_all.at[a, (row + step) % RING, pl.ds(start, long if size is None else size)]
+
+    locals_ = [
+        pltpu.make_async_copy(x_ref, x_all.at[place.col], local_sem.at[0]),
+        pltpu.make_async_copy(bias_ref.at[0], bias_spot(0, 0), local_sem.at[1]),
+    ]
+    for copy in locals_:
+        copy.start()
+
+    odd = links.send(bias_ref.at[1], bias_spot(1, 0), place.partner())
+    bias_direct = {}
+    for step in (1, -1):
+        bias_direct[0, step] = links.send(bias_ref.at[0], bias_spot(0, 0), place.along_x(step))
+    first = {}
+    for hf in range(2):
+        mine = own(hf * half, half)
+        for step in (1, -1):
+            first[hf, step] = links.send(mine, spot((0, 0), hf * half, half), place.along(hf, step))
+    second = {}
+    chip = {}
+
+    def pass_on(hf, offset, src=None):
+        steps = pair_steps(hf, offset, 0)
+        there = spot(steps, hf * half, half)
+        for step in (1, -1):
+            second[hf, offset, step] = links.send(there if src is None else src, there, place.along(1 - hf, step))
+        chip[hf, offset, 0] = links.send(there if src is None else src, there, place.sibling())
+
+    links.arrived(odd, bias_spot(1, 0))
+    for step in (1, -1):
+        bias_direct[1, step] = links.send(bias_spot(1, 0), bias_spot(1, 0), place.along_x(step))
+    bias_onward = {}
+
+    def bias_forward(a):
+        for step in (1, -1):
+            links.arrived(bias_direct[a, step], bias_spot(a, -step))
+            piece = bias_spot(a, -step, 0 if step == 1 else long // 2, long // 2)
+            bias_onward[a, step] = links.send(piece, piece, place.along_x(step))
+
+    for hf in range(2):
+        pass_on(hf, 0, own(hf * half, half))
+    d_move = links.send(d_ref.at[1], d_odd, place.partner())
+
+    onward = {}
+    for step in (1, -1):
+        for hf in range(2):
+            links.arrived(first[hf, step], spot(pair_steps(hf, -step, 0), hf * half, half))
+            begin = hf * half + (0 if step == 1 else sub)
+            piece = spot(pair_steps(hf, -step, 0), begin, sub)
+            onward[hf, step] = links.send(piece, piece, place.along(hf, step))
+            pass_on(hf, -step)
+    for hf in range(2):
+        for step in (1, -1):
+            begin = hf * half + (0 if step == 1 else sub)
+            links.arrived(onward[hf, step], spot(pair_steps(hf, 2, 0), begin, sub))
+        pass_on(hf, 2)
+
+    far = {}
+    for offset in (0, -1, 1, 2):
+        for hf in range(2):
+            for step in (1, -1):
+                steps = pair_steps(hf, offset, -step)
+                links.arrived(second[hf, offset, step], spot(steps, hf * half, half))
+                begin = hf * half + (0 if step == 1 else sub)
+                piece = spot(steps, begin, sub)
+                far[hf, offset, step] = links.send(piece, piece, place.along(1 - hf, step))
+                there = spot(steps, hf * half, half)
+                chip[hf, offset, step] = links.send(there, there, place.sibling())
+        if offset == 0:
+            bias_forward(0)
+        if offset == 1:
+            bias_forward(1)
+    for offset in (0, -1, 1, 2):
+        for hf in range(2):
+            steps = pair_steps(hf, offset, 2)
+            for step in (1, -1):
+                begin = hf * half + (0 if step == 1 else sub)
+                links.arrived(far[hf, offset, step], spot(steps, begin, sub))
+            there = spot(steps, hf * half, half)
+            chip[hf, offset, 2] = links.send(there, there, place.sibling())
+    for a in range(2):
+        for step in (1, -1):
+            begin = 0 if step == 1 else long // 2
+            links.arrived(bias_onward[a, step], bias_spot(a, 2, begin, long // 2))
+    links.arrived(d_move, d_odd)
+    for (hf, offset, step), n in chip.items():
+        steps = pair_steps(hf, offset, -step)
+        links.arrived(n, spot(steps, hf * half, half, 1 - place.core))
+    links.finish()
+    for copy in locals_:
+        copy.wait()
+
+
+def gather(normed, bias_pair, d_out_pair):
+    rows, cols, chans = normed.shape
+    anywhere = pl.BlockSpec(memory_space=pl.ANY)
+    copies = 100
+    return pl.pallas_call(
+        gather_kernel,
+        out_shape=(
+            jax.ShapeDtypeStruct((8 * RING, rows, cols, chans), BF16),
+            jax.ShapeDtypeStruct((2, RING) + bias_pair.shape[1:], BF16),
+            jax.ShapeDtypeStruct(d_out_pair.shape[1:], BF16),
+        ),
+        in_specs=[anywhere] * 3,
+        out_specs=(anywhere,) * 3,
+        scratch_shapes=[
+            pltpu.SemaphoreType.DMA((2,)),
+            pltpu.SemaphoreType.DMA((copies,)),
+            pltpu.SemaphoreType.DMA((copies,)),
+        ],
+        compiler_params=pltpu.CompilerParams(collective_id=0, has_side_effects=True),
+        name="gather",
+    )(normed, bias_pair, d_out_pair)
+
+
+def add_into(dst, *sources):
+    def step(n, _):
+        total = dst[n].astype(F32)
+        for source in sources:
+            total = total + source[n].astype(F32)
+        dst[n] = total.astype(BF16)
+        return 0
+
+    lax.fori_loop(0, dst.shape[0], step, 0)
+
+
+def reduce_kernel(
+    pair_ref, grad_ref, out_ref, dn_ref, pair_sum, grad_all, out_odd, dn_odd,
+    held, chip_in, one_in, two_in, last_one, last_two, grad_held, grad_one, grad_two,
+    local_sem, send_sem, recv_sem, a2a_send, a2a_recv,
+):
+    place = Place()
+    links = Links(send_sem, recv_sem)
+    links.me = place.sibling()
+    row, col = place.row, place.col
+    ncol = grad_all.shape[1]
+    rows = pair_ref.shape[2]
+    sub = rows // 2
+    groups = grad_held.shape[2]
+
+    barrier = pltpu.get_barrier_semaphore()
+
+    def greet_one(d, _):
+        pl.semaphore_signal(barrier, inc=1, device_id=(row, (col + d) % ncol), device_id_type=MESH)
+        return 0
+
+    lax.fori_loop(1, ncol, greet_one, 0)
+    for step in (1, -1):
+        pl.semaphore_signal(barrier, inc=1, device_id=place.along_x(step), device_id_type=MESH)
+    pl.semaphore_wait(barrier, ncol + 1)
+
+    moves = [links.send(out_ref.at[1], out_odd, place.partner()), links.send(dn_ref.at[1], dn_odd, place.partner())]
+
+    def half_of(step):
+        return pl.ds(0 if step == 1 else groups // 2, groups // 2)
+
+    grad_first = {}
+    for a in range(2):
+        for n, step in enumerate((1, -1)):
+            grad_first[a, step] = links.send(
+                grad_ref.at[a, (row + 2) % RING, half_of(step)], grad_one.at[a, n], place.along_x(step)
+            )
+    grad_local = {}
+    for a in range(2):
+        for rel in (1, 3, 0):
+            n = len(grad_local)
+            grad_local[a, rel] = pltpu.make_async_copy(
+                grad_ref.at[a, (row + rel) % RING], grad_held.at[a, rel], local_sem.at[n]
+            )
+            grad_local[a, rel].start()
+
+    def slot(hf, i, b):
+        dy, dz = pair_steps(hf, i, b)
+        return dy, dz, dy * RING + dz
+
+    chip = {}
+    local = {}
+    for b in (2, 1, 3, 0):
+        for hf in range(2):
+            for i in (2, 1, 3, 0):
+                dy, dz, n = slot(hf, i, b)
+                chip[hf, i, b] = links.send(
+                    pair_ref.at[place.col_at((dy, dz), 1 - place.core), hf], chip_in.at[n, hf], place.sibling()
+                )
+                local[hf, i, b] = pltpu.make_async_copy(
+                    pair_ref.at[place.col_at((dy, dz)), hf], held.at[n, hf], local_sem.at[6 + len(local)]
+                )
+                local[hf, i, b].start()
+
+    def collect(hf, i, b):
+        n = slot(hf, i, b)[2]
+        local[hf, i, b].wait()
+        links.arrived(chip[hf, i, b], chip_in.at[n, hf])
+        add_into(held.at[n, hf], chip_in.at[n, hf])
+        return held.at[n, hf]
+
+    def sub_of(step):
+        return pl.ds(0 if step == 1 else sub, sub)
+
+    one = {}
+    for hf in range(2):
+        for i in (2, 1, 3, 0):
+            block = collect(hf, i, 2)
+            for n, step in enumerate((1, -1)):
+                one[hf, i, step] = links.send(
+                    block.at[sub_of(step)], one_in.at[hf, i, n], place.along(1 - hf, step)
+                )
+
+    grad_second = {}
+    for a in range(2):
+        for n, step in enumerate((1, -1)):
+            rel = step % RING
+            grad_local[a, rel].wait()
+            links.arrived(grad_first[a, step], grad_one.at[a, n])
+            add_into(grad_held.at[a, rel, half_of(step)], grad_one.at[a, n])
+            grad_second[a, step] = links.send(grad_held.at[a, rel], grad_two.at[a, n], place.along_x(step))
+
+    two = {}
+    for n, step in enumerate((1, -1)):
+        for hf in range(2):
+            for i in (2, 1, 3, 0):
+                block = collect(hf, i, step % RING)
+                links.arrived(one[hf, i, step], one_in.at[hf, i, n])
+                add_into(block.at[sub_of(step)], one_in.at[hf, i, n])
+                two[hf, i, step] = links.send(block, two_in.at[hf, i, n], place.along(1 - hf, step))
+    mine = {(hf, i): collect(hf, i, 0) for hf in range(2) for i in (2, 1, 3, 0)}
+
+    for a in range(2):
+        grad_local[a, 0].wait()
+        for n, step in enumerate((1, -1)):
+            links.arrived(grad_second[a, step], grad_two.at[a, n])
+        add_into(grad_held.at[a, 0], grad_two.at[a, 0], grad_two.at[a, 1])
+    per = grad_all.shape[2]
+
+    def keys_of(a, device):
+        return grad_held.at[a, 0, pl.ds(device * per, per)]
+
+    def a2a(a, d):
+        target = (col + d) % ncol
+        return pltpu.make_async_remote_copy(
+            src_ref=keys_of(a, target), dst_ref=grad_all.at[a, col],
+            send_sem=a2a_send.at[a, d], recv_sem=a2a_recv.at[a, d],
+            device_id=(row, target), device_id_type=MESH,
+        )
+
+    def a2a_back(a, d):
+        source = (col - d) % ncol
+        return pltpu.make_async_remote_copy(
+            src_ref=keys_of(a, source), dst_ref=grad_all.at[a, source],
+            send_sem=a2a_send.at[a, d], recv_sem=a2a_recv.at[a, d],
+            device_id=(row, source), device_id_type=MESH,
+        )
+
+    def a2a_start(d, _):
+        for a in range(2):
+            a2a(a, d).start()
+        return 0
+
+    lax.fori_loop(1, ncol, a2a_start, 0)
+    keep = [pltpu.make_async_copy(keys_of(a, col), grad_all.at[a, col], local_sem.at[38 + a]) for a in range(2)]
+    for copy in keep:
+        copy.start()
+
+    tail_one, tail_two = {}, {}
+    for i in (2, 1, 3, 0):
+        for hf in range(2):
+            block = mine[hf, i]
+            for n, step in enumerate((1, -1)):
+                links.arrived(two[hf, i, step], two_in.at[hf, i, n])
+            add_into(block, two_in.at[hf, i, 0], two_in.at[hf, i, 1])
+            if i == 2:
+                for n, step in enumerate((1, -1)):
+                    tail_one[hf, step] = links.send(
+                        block.at[sub_of(step)], last_one.at[hf, n], place.along(hf, step)
+                    )
+            elif i != 0:
+                n, step = (0, 1) if i == 1 else (1, -1)
+                links.arrived(tail_one[hf, step], last_one.at[hf, n])
+                add_into(block.at[sub_of(step)], last_one.at[hf, n])
+                tail_two[hf, step] = links.send(block, last_two.at[hf, n], place.along(hf, step))
+    for hf in range(2):
+        block = mine[hf, 0]
+        for n, step in enumerate((1, -1)):
+            links.arrived(tail_two[hf, step], last_two.at[hf, n])
+        add_into(block, last_two.at[hf, 0], last_two.at[hf, 1])
+        pair_sum[hf] = block[...]
+
+    def a2a_end(d, _):
+        for a in range(2):
+            a2a_back(a, d).wait_recv()
+            a2a(a, d).wait_send()
+        return 0
+
+    lax.fori_loop(1, ncol, a2a_end, 0)
+    links.arrived(moves[0], out_odd)
+    links.arrived(moves[1], dn_odd)
+    links.finish()
+    for copy in keep:
+        copy.wait()
+
+
+def reduce(pair, bias_grad, out, dn):
+    ncol = 8 * RING
+    rows, cols, chans = out.shape[1:]
+    pair = pair.reshape(ncol, 2, rows, cols, chans)
+    keys = bias_grad.shape[1] * TILE // RING
+    unit = 32
+    grads = bias_grad.reshape(2, RING, keys // unit, unit, HJ)
+    part = keys // ncol
+    anywhere = pl.BlockSpec(memory_space=pl.ANY)
+    vmem = pl.BlockSpec(memory_space=pltpu.VMEM)
+    block = (rows, cols, chans)
+    half = (rows // 2, cols, chans)
+    return pl.pallas_call(
+        reduce_kernel,
+        out_shape=(
+            jax.ShapeDtypeStruct((2,) + block, BF16),
+            jax.ShapeDtypeStruct((2, ncol, part // unit, unit, HJ), BF16),
+            jax.ShapeDtypeStruct(block, BF16),
+            jax.ShapeDtypeStruct(block, BF16),
+        ),
+        in_specs=[anywhere] * 4,
+        out_specs=(vmem, anywhere, anywhere, anywhere),
+        scratch_shapes=[
+            pltpu.VMEM((RING * RING, 2) + block, BF16),
+            pltpu.VMEM((RING * RING, 2) + block, BF16),
+            pltpu.VMEM((2, RING, 2) + half, BF16),
+            pltpu.VMEM((2, RING, 2) + block, BF16),
+            pltpu.VMEM((2, 2) + half, BF16),
+            pltpu.VMEM((2, 2) + block, BF16),
+            pltpu.VMEM((2, RING, keys // unit, unit, HJ), BF16),
+            pltpu.VMEM((2, 2, keys // unit // 2, unit, HJ), BF16),
+            pltpu.VMEM((2, 2, keys // unit, unit, HJ), BF16),
+            pltpu.SemaphoreType.DMA((40,)),
+            pltpu.SemaphoreType.DMA((90,)),
+            pltpu.SemaphoreType.DMA((90,)),
+            pltpu.SemaphoreType.DMA((2, ncol)),
+            pltpu.SemaphoreType.DMA((2, ncol)),
+        ],
+        compiler_params=pltpu.CompilerParams(
+            collective_id=1, has_side_effects=True, vmem_limit_bytes=40 * 1024 * 1024
+        ),
+        name="reduce",
+    )(pair, grads, out, dn)
+
+
 def on_device(pair_slab, pair_bias, tile_mask, w_proj, w_out, d_out):
     rows, cols, chans = pair_slab.shape
     ncol = lax.axis_size("col")
-    flip = [(i, ncol - 1 - i) for i in range(ncol)]
     c = lax.axis_index("col")
     entries = pair_slab.astype(F32)
     centred = entries - jnp.mean(entries, axis=-1, keepdims=True)
     spread = jnp.mean(centred * centred, axis=-1, keepdims=True)
     rstd = lax.rsqrt(spread + eps_norm)
     normed_f = centred * rstd
-    x_all = lax.all_gather(normed_f.astype(BF16), "col", axis=0)
+    normed = normed_f.astype(BF16)
 
     halves = pair_bias.reshape(H, 2, TILE, -1).transpose(1, 3, 0, 2).reshape(2, -1, HJ)
-    bias_pair = jnp.stack([halves[0], lax.ppermute(halves[1], "col", flip)])
-    bias_t = lax.all_gather(bias_pair, "row", axis=1, tiled=True)
-    bias_t = bias_t.reshape(2, -1, TILE, HJ)
     d_out_h = d_out.reshape(rows, 2, TILE, chans).transpose(1, 0, 2, 3)
-    d_out_pair = jnp.stack([d_out_h[0], lax.ppermute(d_out_h[1], "col", flip)])
+    x_all, bias_all, d_odd = gather(normed, halves, d_out_h)
+    bias_t = bias_all.reshape(2, -1, TILE, HJ)
+    d_out_pair = jnp.stack([d_out_h[0], d_odd])
 
     out, dn, pair, bias_grad = attention(
         c.reshape(1).astype(jnp.int32), tile_mask, x_all, bias_t, d_out_pair, w_proj, w_out
     )
 
-    out_odd = lax.ppermute(out[1], "col", flip)
+    pair_sum, grads, out_odd, dn_odd = reduce(pair, bias_grad, out, dn)
     attn_out = jnp.stack([out[0], out_odd], axis=1).reshape(rows, cols, chans)
-    dn_odd = lax.ppermute(dn[1], "col", flip)
     dn_own = jnp.stack([dn[0], dn_odd], axis=1).reshape(rows, cols, chans).astype(F32)
-    pair_sum = lax.psum_scatter(pair, "col", scatter_dimension=0, tiled=True)
     pair_sum = pair_sum.transpose(1, 0, 2, 3).reshape(rows, cols, chans)
     d_normed = dn_own + pair_sum.astype(F32)
     slab_grads = rstd * (
@@ -282,10 +717,7 @@
         - jnp.mean(d_normed, axis=-1, keepdims=True)
         - normed_f * jnp.mean(d_normed * normed_f, axis=-1, keepdims=True)
     )
-    grads = bias_grad.reshape(2, -1, HJ)
-    grads = lax.psum_scatter(grads, "row", scatter_dimension=1, tiled=True)
     grads = grads.reshape(2, ncol, -1, H, TILE)
-    grads = lax.all_to_all(grads, "col", split_axis=1, concat_axis=1, tiled=True)
     even = grads[0]
     odd = grads[1][::-1]
     both = jnp.stack([even, odd], axis=1).astype(F32)

time: 403 us -> 252 us (0.63)
  waiting for transfers between devices: 232 us -> 0 us
  Pallas kernels: 88.2 us -> 218 us
  starting transfers between devices: 26.5 us -> 0 us
  between operations: 14 us -> 0.8 us
  local copies, waits for them, and re-layouts: 34.1 us -> 21.3 us
    pallas_call x0 -> x2, Pallas kernels: none -> 123 us  [the longest x1 72.3 us: reduce(): pl.pallas_call(reduce_kernel, out_shape=(jax.ShapeDtypeStruct((2,) + bloc...]
    reduce_scatter x2 -> x0, waiting for transfers between devices: 113 us -> none  [the longest x1 72.7 us: on_device(): grads = lax.psum_scatter(grads, 'row', scatter_dimension=1, tiled=True)]
    all_gather x2 -> x0, waiting for transfers between devices: 88 us -> none  [the longest x1 50.3 us: on_device(): x_all = lax.all_gather(normed_f.astype(BF16), 'col', axis=0)]
    ppermute x4 -> x0, waiting for transfers between devices: 30 us -> none  [the longest x1 14.8 us: on_device(): out_odd = lax.ppermute(out[1], 'col', flip)]
    ppermute x4 -> x0, starting transfers between devices: 18.7 us -> none  [the longest x1 7.68 us: on_device(): bias_pair = jnp.stack([halves[0], lax.ppermute(halves[1], 'col', flip)])]
    unnamed x14 -> x10, local copies, waits for them, and re-layouts: 18.2 us -> 4.1 us
    all_to_all x1 -> x0, starting transfers between devices: 7.65 us -> none  [on_device(): lax.all_to_all(grads, 'col', split_axis=1, concat_axis=1, tiled=True)]
    pallas_call x1, Pallas kernels: 88.2 us -> 95.3 us  [attention(): pl.pallas_call(attention_kernel, out_shape=(jax.ShapeDtypeStruct((2, rows...]
  transfers between devices with their start and end apart: 9 -> 0, of which waited for: 7 -> 0; matrix products, arithmetic and copies ran while one was open for 9% -> 0% of each run, Pallas kernels for 0% -> 0%
where the time goes in v2:
time: 252 us; the launch traced here: 250 us
  Pallas kernels  218 us (87%)
  local copies, waits for them, and re-layouts  21.3 us (8%)
  other arithmetic  9.72 us (4%)
    pallas_call x1, Pallas kernels, attention(): pl.pallas_call(attention_kernel, out_shape=(jax.ShapeDtypeStruct((2, rows...  95.3 us
    pallas_call x1, Pallas kernels, reduce(): pl.pallas_call(reduce_kernel, out_shape=(jax.ShapeDtypeStruct((2,) + bloc...  72.3 us
    pallas_call x1, Pallas kernels, gather(): pl.pallas_call(gather_kernel, out_shape=(jax.ShapeDtypeStruct((8 * RING,...  50.8 us
    reshape x2, local copies, waits for them, and re-layouts, on_device(): bias_grads = both.transpose(2, 3, 0, 1, 4).reshape(-1, H, ncol * cols)  11.3 us

profile of v2, /device:TPU:1, one launch (start us, length us, event | category | flops | bytes accessed | tf_op | source)
XLA Modules:
  0.0 250.3 jit_solution(15297822268031742309)
XLA Ops:
  0.6 1.1 convert_reduce_fusion
  1.7 1.3 fusion.9
  3.1 2.0 fusion.4.x_ref
  5.1 1.0 copy.36
  6.0 0.0 copy-start.4
  6.1 1.4 copy.28
  7.5 1.3 copy.30.bias_ref
  8.8 0.0 copy-done.4
  8.8 50.8 %gather.1 = (bf16[32,8,128,128]{3,2,1,0:T(8,128)(2,1)}, bf16[2,4,1024,256]{3,2,1,0:T(8,128)(2,1)}, bf16[8,64,128]{2,1,0:T(8,128)(2,1)}) custom-call(bf16[8,128,128]{2,1,0:T(8,128)(2,1)} %fusion.4.x_ref, bf16[2,1024,256]{2,1,0:T(8,128)(2,1)} %copy.30.bias_ref, bf16[2,8,64,128]{3,2,1,0:T(8,128)(2,1)} %bitcast.44), custom_call_target="tpu_custom_call" | custom-call | tf_op jit(solution)/shard_map/gather/pallas_call | solution.py:439
  59.7 1.6 pad_maximum_fusion.d_out_ref
  61.3 95.3 %attention.1 = (bf16[2,8,64,128]{3,2,1,0:T(8,128)(2,1)}, bf16[2,8,64,128]{3,2,1,0:T(8,128)(2,1)}, bf16[64,8,64,128]{3,2,1,0:T(8,128)(2,1)}, bf16[2,64,64,256]{3,2,1,0:T(8,128)(2,1)}) custom-call(s32[1]{0:T(128)} %bitcast.place_ref, s32[64,64]{1,0:T(8,128)} %mask_ref.1, bf16[32,8,128,128]{3,2,1,0:T(8,128)(2,1)} %get-tuple-element.14.x_ref, ...), custom_call_target="tpu_custom_call" | custom-call | tf_op jit(solution)/shard_map/attention/pallas_call | solution.py:220
  156.6 0.0 copy-start
  156.6 2.2 copy-done
  158.8 0.0 copy-start.1
  158.8 0.9 copy-done.1
  159.8 0.0 copy-start.2
  159.8 0.9 copy-done.2
  160.7 0.0 copy-start.3
  160.7 72.3 %reduce.2 = (bf16[2,8,64,128]{3,2,1,0:T(8,128)(2,1)S(1)}, bf16[2,32,1,32,256]{4,3,2,1,0:T(8,128)(2,1)S(1)}, bf16[8,64,128]{2,1,0:T(8,128)(2,1)S(1)}, bf16[8,64,128]{2,1,0:T(8,128)(2,1)S(1)}) custom-call(bf16[32,2,8,64,128]{4,3,2,1,0:T(8,128)(2,1)} %bitcast.40, bf16[2,4,32,32,256]{4,3,2,1,0:T(8,128)(2,1)S(1)} %bitcast.37, ...), custom_call_target="tpu_custom_call" | custom-call | tf_op jit(solution)/shard_map/reduce/pallas_call | solution.py:656
  233.1 0.7 copy.31
  233.8 0.2 fusion.10
  234.1 0.1 div.17
  234.2 0.0 copy-done.3
  234.2 0.5 fusion.5
  234.7 1.3 fusion.8
  236.0 0.1 fusion.11
  236.1 0.4 stack_squeeze.11
  236.5 0.4 squeeze.3
  236.9 0.4 reverse_bitcast_fusion
  237.4 1.6 convert_bitcast_fusion
  239.0 5.2 %copy.34 = f32[32,4,32,2,64]{4,3,2,1,0:T(2,128)} copy(f32[32,4,32,2,64]{4,1,0,2,3:T(4,128)S(1)} %convert_bitcast_fusion) | data formatting | bytes 4194304 | tf_op jit(solution)/shard_map/reshape | solution.py:724
  244.1 6.2 %reshape.85 = f32[32,4,4096]{2,1,0:T(4,128)} reshape(f32[32,4,32,2,64]{4,3,2,1,0:T(2,128)} %copy.34) | data formatting | bytes 4194304 | tf_op jit(solution)/shard_map/reshape | solution.py:724
  (9 shorter events, 0.1 us)
Async XLA Ops:
  6.0 2.8 %copy-start.4 = (bf16[8,2,64,128]{3,2,0,1:T(8,128)(2,1)}, bf16[8,2,64,128]{3,2,0,1:T(8,128)(2,1)S(1)}, u32[]{:S(2)}) copy-start(bf16[8,2,64,128]{3,2,0,1:T(8,128)(2,1)S(1)} %copy.36) | copy-start | bytes 786436
  156.6 2.2 copy-start
  158.8 0.9 copy-start.1
  159.8 0.9 copy-start.2
  160.7 73.4 %copy-start.3 = (bf16[8,128,128]{2,1,0:T(8,128)(2,1)S(1)}, bf16[8,128,128]{2,1,0:T(8,128)(2,1)}, u32[]{:S(2)}) copy-start(bf16[8,128,128]{2,1,0:T(8,128)(2,1)} %param.6) | copy-start | bytes 786436

commit v3 on v2

--- a/solution.py
+++ b/solution.py
@@ -14,7 +14,9 @@
 
 eps_norm = 1e-05
 neg_big = -1e30
-CT = 4
+CT = 8
+GROUP = 8
+SKEW = 2
 F32 = jnp.float32
 BF16 = jnp.bfloat16
 
@@ -46,7 +48,7 @@
     place_ref, mask_ref, x_ref, bias_ref, d_out_ref, w_proj_ref, w_out_ref,
     out_ref, dn_ref, pair_ref, bias_grad_ref,
     k_ref, v_ref, q_ref, do_ref, bias_f, grad_f, max_ref, sum_ref, delta_ref, acc_ref,
-    gate_ref, dg_ref, list_ref,
+    gate_ref, dg_ref, list_ref, qt_ref, dt_ref,
 ):
     c = place_ref[0]
     tiles = 2 * x_ref.shape[0]
@@ -57,13 +59,14 @@
     w_q = w_proj_ref[:, :width]
     w_pair = w_proj_ref[:, width : 3 * width]
     w_gate = w_proj_ref[:, 3 * width :]
+    w_pair_t = jnp.transpose(w_pair)
 
     def project(block, _):
-        for r in range(rows):
-            kv = nn(x_ref[block, r], w_pair).astype(BF16)
-            for half in range(2):
-                k_ref[2 * block + half, r] = kv[half * TILE : (half + 1) * TILE, :width]
-                v_ref[2 * block + half, r] = kv[half * TILE : (half + 1) * TILE, width:]
+        kv = nn(x_ref[block].reshape(rows * 2 * TILE, -1), w_pair).astype(BF16)
+        kv = kv.reshape(rows, 2 * TILE, 2 * width)
+        for half in range(2):
+            k_ref[2 * block + half] = kv[:, half * TILE : (half + 1) * TILE, :width]
+            v_ref[2 * block + half] = kv[:, half * TILE : (half + 1) * TILE, width:]
         return 0
 
     lax.fori_loop(0, jnp.maximum(c, tiles // 2 - 1 - c) + 1, project, 0)
@@ -83,23 +86,25 @@
         idles.append(idle)
 
     blocks = head_blocks(HJ, width)
+    zero = jnp.zeros((HJ, width), BF16)
     for a in range(2):
         tile = query_tiles[a]
-
-        def prepare(r, _, a=a, tile=tile):
-            x_q = x_ref[tile // 2, r, pl.ds(pl.multiple_of((tile % 2) * TILE, TILE), TILE), :]
-            queries = (nn(x_q, w_q) * q_scale).astype(BF16)
-            gating = jax.nn.sigmoid(nn(x_q, w_gate))
-            d_gated = nt(d_out_ref[a, r], w_out_ref[...])
-            d_att = (d_gated * gating).astype(BF16)
-            zero = jnp.zeros((HJ, width), BF16)
-            q_ref[a, r] = jnp.where(blocks, jnp.concatenate([queries] * H, axis=0), zero)
-            do_ref[a, r] = jnp.where(blocks, jnp.concatenate([d_att] * H, axis=0), zero)
-            gate_ref[a, r] = gating
-            dg_ref[a, r] = d_gated
-            return 0
-
-        lax.fori_loop(0, rows, prepare, 0)
+        x_q = x_ref[tile // 2, :, pl.ds(pl.multiple_of((tile % 2) * TILE, TILE), TILE), :]
+        x_q = x_q.reshape(rows * TILE, -1)
+        queries = (nn(x_q, w_q) * q_scale).astype(BF16)
+        gating = jax.nn.sigmoid(nn(x_q, w_gate))
+        d_gated = nt(d_out_ref[a].reshape(rows * TILE, -1), w_out_ref[...])
+        d_att = (d_gated * gating).astype(BF16)
+        gate_ref[a] = gating.reshape(rows, TILE, width)
+        dg_ref[a] = d_gated.reshape(rows, TILE, width)
+        for r in range(rows):
+            part = slice(r * TILE, (r + 1) * TILE)
+            q = jnp.where(blocks, jnp.concatenate([queries[part]] * H, axis=0), zero)
+            do = jnp.where(blocks, jnp.concatenate([d_att[part]] * H, axis=0), zero)
+            q_ref[a, r] = q
+            do_ref[a, r] = do
+            qt_ref[a, r] = jnp.transpose(q)
+            dt_ref[a, r] = jnp.transpose(do)
 
     def load_chunk(a, n):
         ids = [list_ref[a, n * CT + t] for t in range(CT)]
@@ -116,10 +121,12 @@
         def forward(n, _, a=a):
             ids = load_chunk(a, n)
 
-            def per_row(r):
+            def score(r):
                 keys = jnp.concatenate([k_ref[i, r] for i in ids], axis=0)
+                return nn(keys, qt_ref[a, r]) + bias_f[...]
+
+            def use(r, scores):
                 values = jnp.concatenate([v_ref[i, r] for i in ids], axis=0)
-                scores = nt(keys, q_ref[a, r]) + bias_f[...]
                 old = max_ref[a, r]
                 new = jnp.maximum(old, jnp.max(scores, axis=0, keepdims=True))
                 fade = jnp.exp(old - new)
@@ -129,32 +136,33 @@
                 acc_ref[a, r] = acc_ref[a, r] * fade + tn(values, probs.astype(BF16))
 
             def some_rows(step, _):
-                for u in range(2):
-                    per_row(step * 2 + u)
+                waiting = []
+                for u in range(GROUP + SKEW):
+                    if u < GROUP:
+                        waiting.append(score(step * GROUP + u))
+                    if u >= SKEW:
+                        use(step * GROUP + u - SKEW, waiting.pop(0))
                 return 0
 
-            lax.fori_loop(0, rows // 2, some_rows, 0)
+            lax.fori_loop(0, rows // GROUP, some_rows, 0)
             return 0
 
         lax.fori_loop(0, (counts[a] + CT - 1) // CT, forward, 0)
 
     for a in range(2):
-        def middle(r, _, a=a):
+        attended = []
+        for r in range(rows):
             total = sum_ref[a, r]
             full_t = acc_ref[a, r] * (1.0 / total)
             max_ref[a, r] = max_ref[a, r] + jnp.log(total)
-            delta_ref[a, r] = jnp.sum(
-                full_t * jnp.transpose(do_ref[a, r].astype(F32)), axis=0, keepdims=True
-            )
-            attended = diagonal(full_t)
-            gating = gate_ref[a, r]
-            gated = (gating * attended).astype(BF16)
-            out_ref[a, r] = nn(gated, w_out_ref[...]).astype(BF16)
-            dg_ref[a, r] = dg_ref[a, r] * attended * gating * (1.0 - gating)
+            delta_ref[a, r] = jnp.sum(full_t * dt_ref[a, r].astype(F32), axis=0, keepdims=True)
+            attended.append(diagonal(full_t))
             acc_ref[a, r] = jnp.zeros(acc_ref.shape[2:], F32)
-            return 0
-
-        lax.fori_loop(0, rows, middle, 0)
+        attended = jnp.concatenate(attended, axis=0).reshape(rows, TILE, width)
+        gating = gate_ref[a]
+        gated = (gating * attended).astype(BF16).reshape(rows * TILE, width)
+        out_ref[a] = nn(gated, w_out_ref[...]).astype(BF16).reshape(rows, TILE, -1)
+        dg_ref[a] = dg_ref[a] * attended * gating * (1.0 - gating)
 
     def clear(b, _):
         pair_ref[b] = jnp.zeros(pair_ref.shape[1:], BF16)
@@ -167,33 +175,41 @@
         def backward(n, _, a=a):
             ids = load_chunk(a, n)
 
-            def per_row(r, first):
+            def score(r):
                 keys = jnp.concatenate([k_ref[i, r] for i in ids], axis=0)
                 values = jnp.concatenate([v_ref[i, r] for i in ids], axis=0)
-                q = q_ref[a, r]
-                do = do_ref[a, r]
-                probs = jnp.exp(nt(keys, q) + bias_f[...] - max_ref[a, r])
-                d_scores = probs * (nt(values, do) - delta_ref[a, r])
+                return nn(keys, qt_ref[a, r]) + bias_f[...], nn(values, dt_ref[a, r])
+
+            def use(r, made, first):
+                scores, d_probs = made
+                keys = jnp.concatenate([k_ref[i, r] for i in ids], axis=0)
+                probs = jnp.exp(scores - max_ref[a, r])
+                d_scores = probs * (d_probs - delta_ref[a, r])
                 if first is None:
                     grad_f[...] += d_scores
                 else:
                     grad_f[...] = jnp.where(first, d_scores, grad_f[...] + d_scores)
                 d_b = d_scores.astype(BF16)
                 acc_ref[a, r] += tn(keys, d_b)
-                d_keys = nn(d_b, q)
-                d_values = nn(probs.astype(BF16), do)
+                d_keys = nn(d_b, q_ref[a, r])
+                d_values = nn(probs.astype(BF16), do_ref[a, r])
                 both = jnp.concatenate([d_keys, d_values], axis=1).astype(BF16)
-                term = nt(both, w_pair)
+                term = nn(both, w_pair_t)
                 for t in range(CT):
                     piece = term[t * TILE : (t + 1) * TILE]
                     pair_ref[ids[t], r] = (pair_ref[ids[t], r].astype(F32) + piece).astype(BF16)
 
             def some_rows(step, _):
-                for u in range(2):
-                    per_row(step * 2 + u, (step == 0) if u == 0 else None)
+                waiting = []
+                for u in range(GROUP + SKEW):
+                    if u < GROUP:
+                        waiting.append(score(step * GROUP + u))
+                    if u >= SKEW:
+                        first = (step == 0) if u == SKEW else None
+                        use(step * GROUP + u - SKEW, waiting.pop(0), first)
                 return 0
 
-            lax.fori_loop(0, rows // 2, some_rows, 0)
+            lax.fori_loop(0, rows // GROUP, some_rows, 0)
             for t in range(CT):
                 target = jnp.where(n * CT + t < counts[a], ids[t], idles[a])
                 bias_grad_ref[a, target] = grad_f[t * TILE : (t + 1) * TILE, :].astype(BF16)
@@ -202,13 +218,10 @@
         lax.fori_loop(0, (counts[a] + CT - 1) // CT, backward, 0)
 
     for a in range(2):
-        def finish(r, _, a=a):
-            d_q = diagonal(acc_ref[a, r]) * q_scale
-            d_q = nt(d_q.astype(BF16), w_q)
-            dn_ref[a, r] = (d_q + nt(dg_ref[a, r].astype(BF16), w_gate)).astype(BF16)
-            return 0
-
-        lax.fori_loop(0, rows, finish, 0)
+        d_q = jnp.concatenate([diagonal(acc_ref[a, r]) for r in range(rows)], axis=0) * q_scale
+        d_gate = dg_ref[a].reshape(rows * TILE, width)
+        total = nt(d_q.astype(BF16), w_q) + nt(d_gate.astype(BF16), w_gate)
+        dn_ref[a] = total.astype(BF16).reshape(rows, TILE, -1)
 
 
 def attention(place, mask, x_all, bias_t, d_out, w_proj, w_out):
@@ -241,6 +254,8 @@
             pltpu.VMEM((2, rows, TILE, width), F32),
             pltpu.VMEM((2, rows, TILE, width), F32),
             pltpu.SMEM((2, tiles + CT), jnp.int32),
+            pltpu.VMEM((2, rows, width, HJ), BF16),
+            pltpu.VMEM((2, rows, width, HJ), BF16),
         ],
         compiler_params=pltpu.CompilerParams(vmem_limit_bytes=60 * 1024 * 1024),
         name="attention",
@@ -463,7 +478,7 @@
         dst[n] = total.astype(BF16)
         return 0
 
-    lax.fori_loop(0, dst.shape[0], step, 0)
+    lax.fori_loop(0, dst.shape[0], step, 0, unroll=4)
 
 
 def reduce_kernel(
@@ -566,42 +581,6 @@
                 add_into(block.at[sub_of(step)], one_in.at[hf, i, n])
                 two[hf, i, step] = links.send(block, two_in.at[hf, i, n], place.along(1 - hf, step))
     mine = {(hf, i): collect(hf, i, 0) for hf in range(2) for i in (2, 1, 3, 0)}
-
-    for a in range(2):
-        grad_local[a, 0].wait()
-        for n, step in enumerate((1, -1)):
-            links.arrived(grad_second[a, step], grad_two.at[a, n])
-        add_into(grad_held.at[a, 0], grad_two.at[a, 0], grad_two.at[a, 1])
-    per = grad_all.shape[2]
-
-    def keys_of(a, device):
-        return grad_held.at[a, 0, pl.ds(device * per, per)]
-
-    def a2a(a, d):
-        target = (col + d) % ncol
-        return pltpu.make_async_remote_copy(
-            src_ref=keys_of(a, target), dst_ref=grad_all.at[a, col],
-            send_sem=a2a_send.at[a, d], recv_sem=a2a_recv.at[a, d],
-            device_id=(row, target), device_id_type=MESH,
-        )
-
-    def a2a_back(a, d):
-        source = (col - d) % ncol
-        return pltpu.make_async_remote_copy(
-            src_ref=keys_of(a, source), dst_ref=grad_all.at[a, source],
-            send_sem=a2a_send.at[a, d], recv_sem=a2a_recv.at[a, d],
-            device_id=(row, source), device_id_type=MESH,
-        )
-
-    def a2a_start(d, _):
-        for a in range(2):
-            a2a(a, d).start()
-        return 0
-
-    lax.fori_loop(1, ncol, a2a_start, 0)
-    keep = [pltpu.make_async_copy(keys_of(a, col), grad_all.at[a, col], local_sem.at[38 + a]) for a in range(2)]
-    for copy in keep:
-        copy.start()
 
     tail_one, tail_two = {}, {}
     for i in (2, 1, 3, 0):
@@ -620,6 +599,42 @@
                 links.arrived(tail_one[hf, step], last_one.at[hf, n])
                 add_into(block.at[sub_of(step)], last_one.at[hf, n])
                 tail_two[hf, step] = links.send(block, last_two.at[hf, n], place.along(hf, step))
+    for a in range(2):
+        grad_local[a, 0].wait()
+        for n, step in enumerate((1, -1)):
+            links.arrived(grad_second[a, step], grad_two.at[a, n])
+        add_into(grad_held.at[a, 0], grad_two.at[a, 0], grad_two.at[a, 1])
+    per = grad_all.shape[2]
+
+    def keys_of(a, device):
+        return grad_held.at[a, 0, pl.ds(device * per, per)]
+
+    def a2a(a, d):
+        target = (col + d) % ncol
+        return pltpu.make_async_remote_copy(
+            src_ref=keys_of(a, target), dst_ref=grad_all.at[a, col],
+            send_sem=a2a_send.at[a, d], recv_sem=a2a_recv.at[a, d],
+            device_id=(row, target), device_id_type=MESH,
+        )
+
+    def a2a_back(a, d):
+        source = (col - d) % ncol
+        return pltpu.make_async_remote_copy(
+            src_ref=keys_of(a, source), dst_ref=grad_all.at[a, source],
+            send_sem=a2a_send.at[a, d], recv_sem=a2a_recv.at[a, d],
+            device_id=(row, source), device_id_type=MESH,
+        )
+
+    def a2a_start(d, _):
+        for a in range(2):
+            a2a(a, d).start()
+        return 0
+
+    lax.fori_loop(1, ncol, a2a_start, 0)
+    keep = [pltpu.make_async_copy(keys_of(a, col), grad_all.at[a, col], local_sem.at[38 + a]) for a in range(2)]
+    for copy in keep:
+        copy.start()
+
     for hf in range(2):
         block = mine[hf, 0]
         for n, step in enumerate((1, -1)):
@@ -686,6 +701,29 @@
     )(pair, grads, out, dn)
 
 
+def layout_kernel(grad_ref, out_ref):
+    count = grad_ref.shape[1]
+    for m in range(count):
+        even = grad_ref[0, m].astype(F32)
+        odd = grad_ref[1, count - 1 - m].astype(F32)
+        for h in range(H):
+            part = slice(h * TILE, (h + 1) * TILE)
+            both = jnp.concatenate([even[:, part], odd[:, part]], axis=1)
+            out_ref[:, h, 2 * TILE * m : 2 * TILE * (m + 1)] = both
+
+
+def layout(grads):
+    count, keys = grads.shape[1:3]
+    vmem = pl.BlockSpec(memory_space=pltpu.VMEM)
+    return pl.pallas_call(
+        layout_kernel,
+        out_shape=jax.ShapeDtypeStruct((keys, H, 2 * TILE * count), F32),
+        in_specs=[vmem],
+        out_specs=vmem,
+        name="layout",
+    )(grads)
+
+
 def on_device(pair_slab, pair_bias, tile_mask, w_proj, w_out, d_out):
     rows, cols, chans = pair_slab.shape
     ncol = lax.axis_size("col")
@@ -717,11 +755,7 @@
         - jnp.mean(d_normed, axis=-1, keepdims=True)
         - normed_f * jnp.mean(d_normed * normed_f, axis=-1, keepdims=True)
     )
-    grads = grads.reshape(2, ncol, -1, H, TILE)
-    even = grads[0]
-    odd = grads[1][::-1]
-    both = jnp.stack([even, odd], axis=1).astype(F32)
-    bias_grads = both.transpose(2, 3, 0, 1, 4).reshape(-1, H, ncol * cols)
+    bias_grads = layout(grads.reshape(2, ncol, -1, HJ))
     return attn_out, slab_grads.astype(BF16), bias_grads
 
 

time: 252 us -> 189 us (0.75)
  Pallas kernels: 218 us -> 168 us
  local copies, waits for them, and re-layouts: 21.3 us -> 9.64 us
    pallas_call x1, Pallas kernels: 95.3 us -> 50.8 us  [attention(): pl.pallas_call(attention_kernel, out_shape=(jax.ShapeDtypeStruct((2, rows...]
    reshape x2 -> x0, local copies, waits for them, and re-layouts: 11.3 us -> none  [on_device(): bias_grads = both.transpose(2, 3, 0, 1, 4).reshape(-1, H, ncol * cols)]
    pallas_call x1, Pallas kernels: 72.3 us -> 61.8 us  [reduce(): pl.pallas_call(reduce_kernel, out_shape=(jax.ShapeDtypeStruct((2,) + bloc...]
    pallas_call x0 -> x1, Pallas kernels: none -> 4.68 us  [layout(): pl.pallas_call(layout_kernel, out_shape=jax.ShapeDtypeStruct((keys, H, 2...]
    unnamed x10 -> x12, local copies, waits for them, and re-layouts: 4.1 us -> 5.08 us
where the time goes in v3:
time: 189 us; the launch traced here: 187 us
  Pallas kernels  168 us (89%)
  local copies, waits for them, and re-layouts  9.64 us (5%)
  other arithmetic  8.11 us (4%)
    pallas_call x1, Pallas kernels, reduce(): pl.pallas_call(reduce_kernel, out_shape=(jax.ShapeDtypeStruct((2,) + bloc...  61.8 us
    pallas_call x1, Pallas kernels, gather(): pl.pallas_call(gather_kernel, out_shape=(jax.ShapeDtypeStruct((8 * RING,...  50.8 us
    pallas_call x1, Pallas kernels, attention(): pl.pallas_call(attention_kernel, out_shape=(jax.ShapeDtypeStruct((2, rows...  50.8 us
    unnamed x12, local copies, waits for them, and re-layouts  5.08 us
    pallas_call x1, Pallas kernels, layout(): pl.pallas_call(layout_kernel, out_shape=jax.ShapeDtypeStruct((keys, H, 2...  4.68 us

profile of v3, /device:TPU:1, one launch (start us, length us, event | category | flops | bytes accessed | tf_op | source)
XLA Modules:
  0.0 186.7 jit_solution(7722123268603243024)
XLA Ops:
  0.6 1.1 convert_reduce_fusion
  1.7 1.3 fusion.9
  3.1 2.0 %fusion.4.x_ref = bf16[8,128,128]{2,1,0:T(8,128)(2,1)} fusion(bf16[8,128,128]{2,1,0:T(8,128)(2,1)} %param.6, f32[8,128]{1,0:T(8,128)S(1)} %add_rsqrt_fusion, f32[8,128]{1,0:T(8,128)S(1)} %broadcast_multiply_fusion.2), kind=kLoop, calls=%fused_computation.6 | loop fusion | flops 524288 | bytes 532480 | tf_op jit(solution)/shard_map/convert_element_type | solution.py:736
  5.1 1.0 copy.31
  6.0 0.0 copy-start.5
  6.1 1.4 copy.24
  7.5 1.3 copy.26.bias_ref
  8.8 0.0 copy-done.5
  8.8 50.8 %gather.1 = (bf16[32,8,128,128]{3,2,1,0:T(8,128)(2,1)}, bf16[2,4,1024,256]{3,2,1,0:T(8,128)(2,1)}, bf16[8,64,128]{2,1,0:T(8,128)(2,1)}) custom-call(bf16[8,128,128]{2,1,0:T(8,128)(2,1)} %fusion.4.x_ref, bf16[2,1024,256]{2,1,0:T(8,128)(2,1)} %copy.26.bias_ref, bf16[2,8,64,128]{3,2,1,0:T(8,128)(2,1)} %bitcast.38), custom_call_target="tpu_custom_call" | custom-call | tf_op jit(solution)/shard_map/gather/pallas_call | solution.py:454
  59.7 1.6 pad_maximum_fusion.d_out_ref
  61.3 50.8 %attention.1 = (bf16[2,8,64,128]{3,2,1,0:T(8,128)(2,1)}, bf16[2,8,64,128]{3,2,1,0:T(8,128)(2,1)}, bf16[64,8,64,128]{3,2,1,0:T(8,128)(2,1)}, bf16[2,64,64,256]{3,2,1,0:T(8,128)(2,1)}) custom-call(s32[1]{0:T(128)} %bitcast.place_ref, s32[64,64]{1,0:T(8,128)} %mask_ref.1, bf16[32,8,128,128]{3,2,1,0:T(8,128)(2,1)} %get-tuple-element.14.x_ref, ...), custom_call_target="tpu_custom_call" | custom-call | tf_op jit(solution)/shard_map/attention/pallas_call | solution.py:233
  112.1 0.0 copy-start
  112.1 2.2 %copy-done = bf16[2,64,64,256]{3,2,1,0:T(8,128)(2,1)S(1)} copy-done((bf16[2,64,64,256]{3,2,1,0:T(8,128)(2,1)S(1)}, bf16[2,64,64,256]{3,2,1,0:T(8,128)(2,1)}, u32[]{:S(2)}) %copy-start) | copy-done | bytes 4194328
  114.3 0.0 copy-start.2
  114.3 0.9 copy-done.2
  115.2 0.0 copy-start.3
  115.2 0.9 copy-done.3
  116.2 0.0 copy-start.4
  116.2 61.8 %reduce.2 = (bf16[2,8,64,128]{3,2,1,0:T(8,128)(2,1)S(1)}, bf16[2,32,1,32,256]{4,3,2,1,0:T(8,128)(2,1)S(1)}, bf16[8,64,128]{2,1,0:T(8,128)(2,1)S(1)}, bf16[8,64,128]{2,1,0:T(8,128)(2,1)S(1)}) custom-call(bf16[32,2,8,64,128]{4,3,2,1,0:T(8,128)(2,1)} %bitcast.34, bf16[2,4,32,32,256]{4,3,2,1,0:T(8,128)(2,1)S(1)} %bitcast.30, ...), custom_call_target="tpu_custom_call" | custom-call | tf_op jit(solution)/shard_map/reduce/pallas_call | solution.py:671
  178.0 0.0 copy-start.1
  178.0 1.0 copy-done.1
  179.1 0.7 copy.27
  179.8 0.2 fusion.10
  180.0 0.1 div.17
  180.1 0.0 copy-done.4
  180.2 0.5 fusion.5
  180.7 1.3 fusion.8
  182.0 4.7 %layout.1 = f32[32,4,4096]{2,1,0:T(4,128)} custom-call(bf16[2,32,32,256]{3,2,1,0:T(8,128)(2,1)} %bitcast.31), custom_call_target="tpu_custom_call" | custom-call | tf_op jit(solution)/shard_map/layout/pallas_call | solution.py:718
  (9 shorter events, 0.1 us)
Async XLA Ops:
  6.0 2.8 %copy-start.5 = (bf16[8,2,64,128]{3,2,0,1:T(8,128)(2,1)}, bf16[8,2,64,128]{3,2,0,1:T(8,128)(2,1)S(1)}, u32[]{:S(2)}) copy-start(bf16[8,2,64,128]{3,2,0,1:T(8,128)(2,1)S(1)} %copy.31) | copy-start | bytes 786436
  112.1 2.2 %copy-start = (bf16[2,64,64,256]{3,2,1,0:T(8,128)(2,1)S(1)}, bf16[2,64,64,256]{3,2,1,0:T(8,128)(2,1)}, u32[]{:S(2)}) copy-start(bf16[2,64,64,256]{3,2,1,0:T(8,128)(2,1)} %get-tuple-element.19) | copy-start | bytes 12582916
  114.3 0.9 copy-start.2
  115.2 0.9 copy-start.3
  116.2 64.0 %copy-start.4 = (bf16[8,128,128]{2,1,0:T(8,128)(2,1)S(1)}, bf16[8,128,128]{2,1,0:T(8,128)(2,1)}, u32[]{:S(2)}) copy-start(bf16[8,128,128]{2,1,0:T(8,128)(2,1)} %param.6) | copy-start | bytes 786436
  178.0 1.0 copy-start.1

commit v4 on v3

--- a/solution.py
+++ b/solution.py
@@ -45,13 +45,33 @@
 
 
 def attention_kernel(
-    place_ref, mask_ref, x_ref, bias_ref, d_out_ref, w_proj_ref, w_out_ref,
-    out_ref, dn_ref, pair_ref, bias_grad_ref,
+    place_ref, mask_ref, x_far, bias_far, d_out_ref, w_proj_ref, w_out_ref,
+    out_ref, dn_ref, pair_far, bias_grad_far,
+    x_ref, bias_ref, pair_ref, bias_grad_ref, x_sem, move_sem,
     k_ref, v_ref, q_ref, do_ref, bias_f, grad_f, max_ref, sum_ref, delta_ref, acc_ref,
     gate_ref, dg_ref, list_ref, qt_ref, dt_ref,
 ):
     c = place_ref[0]
     tiles = 2 * x_ref.shape[0]
+    used = jnp.maximum(c, tiles // 2 - 1 - c) + 1
+
+    def fetch(block):
+        return pltpu.make_async_copy(x_far.at[block], x_ref.at[block], x_sem.at[block])
+
+    def fetch_start(block, _):
+        fetch(block).start()
+        return 0
+
+    lax.fori_loop(0, used, fetch_start, 0)
+    bias_moves = [
+        pltpu.make_async_copy(bias_far.at[a], bias_ref.at[a], move_sem.at[a]) for a in range(2)
+    ]
+    grad_moves = [
+        pltpu.make_async_copy(bias_grad_ref.at[a], bias_grad_far.at[a], move_sem.at[2 + a]) for a in range(2)
+    ]
+    pair_move = pltpu.make_async_copy(pair_ref, pair_far, move_sem.at[4])
+    for move in bias_moves:
+        move.start()
     rows = x_ref.shape[1]
     width = H * DH
     q_scale = DH ** (-0.5)
@@ -61,7 +81,16 @@
     w_gate = w_proj_ref[:, 3 * width :]
     w_pair_t = jnp.transpose(w_pair)
 
+    def clear(b, _):
+        pair_ref[b] = jnp.zeros(pair_ref.shape[1:], BF16)
+        for a in range(2):
+            bias_grad_ref[a, b] = jnp.zeros(bias_grad_ref.shape[2:], BF16)
+        return 0
+
+    lax.fori_loop(0, tiles, clear, 0)
+
     def project(block, _):
+        fetch(block).wait()
         kv = nn(x_ref[block].reshape(rows * 2 * TILE, -1), w_pair).astype(BF16)
         kv = kv.reshape(rows, 2 * TILE, 2 * width)
         for half in range(2):
@@ -69,7 +98,7 @@
             v_ref[2 * block + half] = kv[:, half * TILE : (half + 1) * TILE, width:]
         return 0
 
-    lax.fori_loop(0, jnp.maximum(c, tiles // 2 - 1 - c) + 1, project, 0)
+    lax.fori_loop(0, used, project, 0)
 
     counts, idles = [], []
     for a in range(2):
@@ -106,48 +135,61 @@
             qt_ref[a, r] = jnp.transpose(q)
             dt_ref[a, r] = jnp.transpose(do)
 
-    def load_chunk(a, n):
-        ids = [list_ref[a, n * CT + t] for t in range(CT)]
-        for t in range(CT):
+    def load_chunk(a, start, ct):
+        ids = [list_ref[a, start + t] for t in range(ct)]
+        for t in range(ct):
             block = bias_ref[a, ids[t]].astype(F32)
-            shut = jnp.where(n * CT + t < counts[a], 0.0, neg_big)
+            shut = jnp.where(start + t < counts[a], 0.0, neg_big)
             bias_f[t * TILE : (t + 1) * TILE, :] = block + shut
         return ids
+
+    def walk(a, chunk):
+        full = (counts[a] + CT // 2 - 1) // CT
+
+        def step(n, _):
+            chunk(a, n * CT, CT)
+            return 0
+
+        lax.fori_loop(0, full, step, 0)
+
+        @pl.when(counts[a] > full * CT)
+        def _():
+            chunk(a, full * CT, CT // 2)
 
     max_ref[...] = jnp.full(max_ref.shape, neg_big, F32)
     sum_ref[...] = jnp.zeros(sum_ref.shape, F32)
     acc_ref[...] = jnp.zeros(acc_ref.shape, F32)
-    for a in range(2):
-        def forward(n, _, a=a):
-            ids = load_chunk(a, n)
-
-            def score(r):
-                keys = jnp.concatenate([k_ref[i, r] for i in ids], axis=0)
-                return nn(keys, qt_ref[a, r]) + bias_f[...]
-
-            def use(r, scores):
-                values = jnp.concatenate([v_ref[i, r] for i in ids], axis=0)
-                old = max_ref[a, r]
-                new = jnp.maximum(old, jnp.max(scores, axis=0, keepdims=True))
-                fade = jnp.exp(old - new)
-                probs = jnp.exp(scores - new)
-                max_ref[a, r] = new
-                sum_ref[a, r] = sum_ref[a, r] * fade + jnp.sum(probs, axis=0, keepdims=True)
-                acc_ref[a, r] = acc_ref[a, r] * fade + tn(values, probs.astype(BF16))
-
-            def some_rows(step, _):
-                waiting = []
-                for u in range(GROUP + SKEW):
-                    if u < GROUP:
-                        waiting.append(score(step * GROUP + u))
-                    if u >= SKEW:
-                        use(step * GROUP + u - SKEW, waiting.pop(0))
-                return 0
-
-            lax.fori_loop(0, rows // GROUP, some_rows, 0)
+    def forward(a, start, ct):
+        ids = load_chunk(a, start, ct)
+
+        def score(r):
+            keys = jnp.concatenate([k_ref[i, r] for i in ids], axis=0)
+            return nn(keys, qt_ref[a, r]) + bias_f[: ct * TILE, :]
+
+        def use(r, scores):
+            values = jnp.concatenate([v_ref[i, r] for i in ids], axis=0)
+            old = max_ref[a, r]
+            new = jnp.maximum(old, jnp.max(scores, axis=0, keepdims=True))
+            fade = jnp.exp(old - new)
+            probs = jnp.exp(scores - new)
+            max_ref[a, r] = new
+            sum_ref[a, r] = sum_ref[a, r] * fade + jnp.sum(probs, axis=0, keepdims=True)
+            acc_ref[a, r] = acc_ref[a, r] * fade + tn(values, probs.astype(BF16))
+
+        def some_rows(step, _):
+            waiting = []
+            for u in range(GROUP + SKEW):
+                if u < GROUP:
+                    waiting.append(score(step * GROUP + u))
+                if u >= SKEW:
+                    use(step * GROUP + u - SKEW, waiting.pop(0))
             return 0
 
-        lax.fori_loop(0, (counts[a] + CT - 1) // CT, forward, 0)
+        lax.fori_loop(0, rows // GROUP, some_rows, 0)
+
+    for a in range(2):
+        bias_moves[a].wait()
+        walk(a, forward)
 
     for a in range(2):
         attended = []
@@ -164,64 +206,60 @@
         out_ref[a] = nn(gated, w_out_ref[...]).astype(BF16).reshape(rows, TILE, -1)
         dg_ref[a] = dg_ref[a] * attended * gating * (1.0 - gating)
 
-    def clear(b, _):
-        pair_ref[b] = jnp.zeros(pair_ref.shape[1:], BF16)
-        for a in range(2):
-            bias_grad_ref[a, b] = jnp.zeros(bias_grad_ref.shape[2:], BF16)
-        return 0
-
-    lax.fori_loop(0, tiles, clear, 0)
-    for a in range(2):
-        def backward(n, _, a=a):
-            ids = load_chunk(a, n)
-
-            def score(r):
-                keys = jnp.concatenate([k_ref[i, r] for i in ids], axis=0)
-                values = jnp.concatenate([v_ref[i, r] for i in ids], axis=0)
-                return nn(keys, qt_ref[a, r]) + bias_f[...], nn(values, dt_ref[a, r])
-
-            def use(r, made, first):
-                scores, d_probs = made
-                keys = jnp.concatenate([k_ref[i, r] for i in ids], axis=0)
-                probs = jnp.exp(scores - max_ref[a, r])
-                d_scores = probs * (d_probs - delta_ref[a, r])
-                if first is None:
-                    grad_f[...] += d_scores
-                else:
-                    grad_f[...] = jnp.where(first, d_scores, grad_f[...] + d_scores)
-                d_b = d_scores.astype(BF16)
-                acc_ref[a, r] += tn(keys, d_b)
-                d_keys = nn(d_b, q_ref[a, r])
-                d_values = nn(probs.astype(BF16), do_ref[a, r])
-                both = jnp.concatenate([d_keys, d_values], axis=1).astype(BF16)
-                term = nn(both, w_pair_t)
-                for t in range(CT):
-                    piece = term[t * TILE : (t + 1) * TILE]
-                    pair_ref[ids[t], r] = (pair_ref[ids[t], r].astype(F32) + piece).astype(BF16)
-
-            def some_rows(step, _):
-                waiting = []
-                for u in range(GROUP + SKEW):
-                    if u < GROUP:
-                        waiting.append(score(step * GROUP + u))
-                    if u >= SKEW:
-                        first = (step == 0) if u == SKEW else None
-                        use(step * GROUP + u - SKEW, waiting.pop(0), first)
-                return 0
-
-            lax.fori_loop(0, rows // GROUP, some_rows, 0)
-            for t in range(CT):
-                target = jnp.where(n * CT + t < counts[a], ids[t], idles[a])
-                bias_grad_ref[a, target] = grad_f[t * TILE : (t + 1) * TILE, :].astype(BF16)
+    def backward(a, start, ct):
+        ids = load_chunk(a, start, ct)
+
+        def score(r):
+            keys = jnp.concatenate([k_ref[i, r] for i in ids], axis=0)
+            values = jnp.concatenate([v_ref[i, r] for i in ids], axis=0)
+            return nn(keys, qt_ref[a, r]) + bias_f[: ct * TILE, :], nn(values, dt_ref[a, r])
+
+        def use(r, made, first):
+            scores, d_probs = made
+            keys = jnp.concatenate([k_ref[i, r] for i in ids], axis=0)
+            probs = jnp.exp(scores - max_ref[a, r])
+            d_scores = probs * (d_probs - delta_ref[a, r])
+            if first is None:
+                grad_f[: ct * TILE, :] += d_scores
+            else:
+                grad_f[: ct * TILE, :] = jnp.where(first, d_scores, grad_f[: ct * TILE, :] + d_scores)
+            d_b = d_scores.astype(BF16)
+            acc_ref[a, r] += tn(keys, d_b)
+            d_keys = nn(d_b, q_ref[a, r])
+            d_values = nn(probs.astype(BF16), do_ref[a, r])
+            both = jnp.concatenate([d_keys, d_values], axis=1).astype(BF16)
+            term = nn(both, w_pair_t)
+            for t in range(ct):
+                piece = term[t * TILE : (t + 1) * TILE]
+                pair_ref[ids[t], r] = (pair_ref[ids[t], r].astype(F32) + piece).astype(BF16)
+
+        def some_rows(step, _):
+            waiting = []
+            for u in range(GROUP + SKEW):
+                if u < GROUP:
+                    waiting.append(score(step * GROUP + u))
+                if u >= SKEW:
+                    first = (step == 0) if u == SKEW else None
+                    use(step * GROUP + u - SKEW, waiting.pop(0), first)
             return 0
 
-        lax.fori_loop(0, (counts[a] + CT - 1) // CT, backward, 0)
+        lax.fori_loop(0, rows // GROUP, some_rows, 0)
+        for t in range(ct):
+            target = jnp.where(start + t < counts[a], ids[t], idles[a])
+            bias_grad_ref[a, target] = grad_f[t * TILE : (t + 1) * TILE, :].astype(BF16)
+
+    for a in range(2):
+        walk(a, backward)
+        grad_moves[a].start()
+    pair_move.start()
 
     for a in range(2):
         d_q = jnp.concatenate([diagonal(acc_ref[a, r]) for r in range(rows)], axis=0) * q_scale
         d_gate = dg_ref[a].reshape(rows * TILE, width)
         total = nt(d_q.astype(BF16), w_q) + nt(d_gate.astype(BF16), w_gate)
         dn_ref[a] = total.astype(BF16).reshape(rows, TILE, -1)
+    for move in grad_moves + [pair_move]:
+        move.wait()
 
 
 def attention(place, mask, x_all, bias_t, d_out, w_proj, w_out):
@@ -230,6 +268,7 @@
     width = H * DH
     vmem = pl.BlockSpec(memory_space=pltpu.VMEM)
     smem = pl.BlockSpec(memory_space=pltpu.SMEM)
+    anywhere = pl.BlockSpec(memory_space=pl.ANY)
     return pl.pallas_call(
         attention_kernel,
         out_shape=(
@@ -238,9 +277,15 @@
             jax.ShapeDtypeStruct((tiles, rows, TILE, chans), BF16),
             jax.ShapeDtypeStruct((2, tiles, TILE, HJ), BF16),
         ),
-        in_specs=[smem, smem, vmem, vmem, vmem, vmem, vmem],
-        out_specs=(vmem,) * 4,
+        in_specs=[smem, smem, anywhere, anywhere, vmem, vmem, vmem],
+        out_specs=(vmem, vmem, anywhere, anywhere),
         scratch_shapes=[
+            pltpu.VMEM(x_all.shape, BF16),
+            pltpu.VMEM(bias_t.shape, BF16),
+            pltpu.VMEM((tiles, rows, TILE, chans), BF16),
+            pltpu.VMEM((2, tiles, TILE, HJ), BF16),
+            pltpu.SemaphoreType.DMA((blocks,)),
+            pltpu.SemaphoreType.DMA((5,)),
             pltpu.VMEM((tiles, rows, TILE, width), BF16),
             pltpu.VMEM((tiles, rows, TILE, width), BF16),
             pltpu.VMEM((2, rows, HJ, width), BF16),
@@ -257,7 +302,7 @@
             pltpu.VMEM((2, rows, width, HJ), BF16),
             pltpu.VMEM((2, rows, width, HJ), BF16),
         ],
-        compiler_params=pltpu.CompilerParams(vmem_limit_bytes=60 * 1024 * 1024),
+        compiler_params=pltpu.CompilerParams(vmem_limit_bytes=62 * 1024 * 1024),
         name="attention",
     )(place, mask, x_all, bias_t, d_out, w_proj, w_out)
 
@@ -582,6 +627,45 @@
                 two[hf, i, step] = links.send(block, two_in.at[hf, i, n], place.along(1 - hf, step))
     mine = {(hf, i): collect(hf, i, 0) for hf in range(2) for i in (2, 1, 3, 0)}
 
+    per = grad_all.shape[2]
+
+    def keys_of(a, device):
+        return grad_held.at[a, 0, pl.ds(device * per, per)]
+
+    def a2a(a, d):
+        target = (col + d) % ncol
+        return pltpu.make_async_remote_copy(
+            src_ref=keys_of(a, target), dst_ref=grad_all.at[a, col],
+            send_sem=a2a_send.at[a, d], recv_sem=a2a_recv.at[a, d],
+            device_id=(row, target), device_id_type=MESH,
+        )
+
+    def a2a_back(a, d):
+        source = (col - d) % ncol
+        return pltpu.make_async_remote_copy(
+            src_ref=keys_of(a, source), dst_ref=grad_all.at[a, source],
+            send_sem=a2a_send.at[a, d], recv_sem=a2a_recv.at[a, d],
+            device_id=(row, source), device_id_type=MESH,
+        )
+
+    keep = []
+
+    def finish_bias(a):
+        grad_local[a, 0].wait()
+        for n, step in enumerate((1, -1)):
+            links.arrived(grad_second[a, step], grad_two.at[a, n])
+        add_into(grad_held.at[a, 0], grad_two.at[a, 0], grad_two.at[a, 1])
+
+        def start(d, _):
+            a2a(a, d).start()
+            return 0
+
+        lax.fori_loop(1, ncol, start, 0)
+        keep.append(pltpu.make_async_copy(keys_of(a, col), grad_all.at[a, col], local_sem.at[38 + a]))
+        keep[-1].start()
+
+    finish_bias(0)
+
     tail_one, tail_two = {}, {}
     for i in (2, 1, 3, 0):
         for hf in range(2):
@@ -599,41 +683,7 @@
                 links.arrived(tail_one[hf, step], last_one.at[hf, n])
                 add_into(block.at[sub_of(step)], last_one.at[hf, n])
                 tail_two[hf, step] = links.send(block, last_two.at[hf, n], place.along(hf, step))
-    for a in range(2):
-        grad_local[a, 0].wait()
-        for n, step in enumerate((1, -1)):
-            links.arrived(grad_second[a, step], grad_two.at[a, n])
-        add_into(grad_held.at[a, 0], grad_two.at[a, 0], grad_two.at[a, 1])
-    per = grad_all.shape[2]
-
-    def keys_of(a, device):
-        return grad_held.at[a, 0, pl.ds(device * per, per)]
-
-    def a2a(a, d):
-        target = (col + d) % ncol
-        return pltpu.make_async_remote_copy(
-            src_ref=keys_of(a, target), dst_ref=grad_all.at[a, col],
-            send_sem=a2a_send.at[a, d], recv_sem=a2a_recv.at[a, d],
-            device_id=(row, target), device_id_type=MESH,
-        )
-
-    def a2a_back(a, d):
-        source = (col - d) % ncol
-        return pltpu.make_async_remote_copy(
-            src_ref=keys_of(a, source), dst_ref=grad_all.at[a, source],
-            send_sem=a2a_send.at[a, d], recv_sem=a2a_recv.at[a, d],
-            device_id=(row, source), device_id_type=MESH,
-        )
-
-    def a2a_start(d, _):
-        for a in range(2):
-            a2a(a, d).start()
-        return 0
-
-    lax.fori_loop(1, ncol, a2a_start, 0)
-    keep = [pltpu.make_async_copy(keys_of(a, col), grad_all.at[a, col], local_sem.at[38 + a]) for a in range(2)]
-    for copy in keep:
-        copy.start()
+    finish_bias(1)
 
     for hf in range(2):
         block = mine[hf, 0]
@@ -695,7 +745,7 @@
             pltpu.SemaphoreType.DMA((2, ncol)),
         ],
         compiler_params=pltpu.CompilerParams(
-            collective_id=1, has_side_effects=True, vmem_limit_bytes=40 * 1024 * 1024
+            collective_id=1, has_side_effects=True, vmem_limit_bytes=62 * 1024 * 1024
         ),
         name="reduce",
     )(pair, grads, out, dn)

time: 189 us -> 175 us (0.926); the launches traced: 187 us -> 175 us
  Pallas kernels: 168 us -> 159 us
  local copies, waits for them, and re-layouts: 9.64 us -> 4.58 us
  other arithmetic: 8.11 us -> 10 us
    unnamed x12 -> x8, local copies, waits for them, and re-layouts: 5.08 us -> 0.03 us
    pallas_call x1, Pallas kernels: 50.8 us -> 46.1 us  [attention(): pl.pallas_call(attention_kernel, out_shape=(jax.ShapeDtypeStruct((2, rows...]
    pallas_call x1, Pallas kernels: 61.8 us -> 57.6 us  [reduce(): pl.pallas_call(reduce_kernel, out_shape=(jax.ShapeDtypeStruct((2,) + bloc...]
where the time goes in v4:
time: 175 us
  Pallas kernels  159 us (91%)
  other arithmetic  10 us (6%)
  local copies, waits for them, and re-layouts  4.58 us (3%)
    pallas_call x1, Pallas kernels, reduce(): pl.pallas_call(reduce_kernel, out_shape=(jax.ShapeDtypeStruct((2,) + bloc...  57.6 us
    pallas_call x1, Pallas kernels, gather(): pl.pallas_call(gather_kernel, out_shape=(jax.ShapeDtypeStruct((8 * RING,...  50.8 us
    pallas_call x1, Pallas kernels, attention(): pl.pallas_call(attention_kernel, out_shape=(jax.ShapeDtypeStruct((2, rows...  46.1 us
    pallas_call x1, Pallas kernels, layout(): pl.pallas_call(layout_kernel, out_shape=jax.ShapeDtypeStruct((keys, H, 2...  4.68 us

profile of v4, /device:TPU:1, one launch (start us, length us, event | category | flops | bytes accessed | tf_op | source)
XLA Modules:
  0.0 174.6 jit_solution(15330770703645301861)
XLA Ops:
  0.6 1.1 convert_reduce_fusion
  1.7 1.3 fusion.9
  3.1 2.0 %fusion.4.x_ref = bf16[8,128,128]{2,1,0:T(8,128)(2,1)} fusion(bf16[8,128,128]{2,1,0:T(8,128)(2,1)} %param.6, f32[8,128]{1,0:T(8,128)S(1)} %add_rsqrt_fusion, f32[8,128]{1,0:T(8,128)S(1)} %broadcast_multiply_fusion.2), kind=kLoop, calls=%fused_computation.6 | loop fusion | flops 524288 | bytes 532480 | tf_op jit(solution)/shard_map/convert_element_type | solution.py:786
  5.1 1.0 copy.31
  6.0 0.0 copy-start.1
  6.1 1.4 copy.24
  7.5 1.3 copy.26.bias_ref
  8.8 0.0 copy-done.1
  8.8 50.8 %gather.1 = (bf16[32,8,128,128]{3,2,1,0:T(8,128)(2,1)}, bf16[2,4,1024,256]{3,2,1,0:T(8,128)(2,1)}, bf16[8,64,128]{2,1,0:T(8,128)(2,1)}) custom-call(bf16[8,128,128]{2,1,0:T(8,128)(2,1)} %fusion.4.x_ref, bf16[2,1024,256]{2,1,0:T(8,128)(2,1)} %copy.26.bias_ref, bf16[2,8,64,128]{3,2,1,0:T(8,128)(2,1)} %bitcast.35), custom_call_target="tpu_custom_call" | custom-call | tf_op jit(solution)/shard_map/gather/pallas_call | solution.py:499
  59.7 1.6 pad_maximum_fusion.d_out_ref
  61.3 46.1 %attention.1 = (bf16[2,8,64,128]{3,2,1,0:T(8,128)(2,1)}, bf16[2,8,64,128]{3,2,1,0:T(8,128)(2,1)}, bf16[64,8,64,128]{3,2,1,0:T(8,128)(2,1)}, bf16[2,64,64,256]{3,2,1,0:T(8,128)(2,1)}) custom-call(s32[1]{0:T(128)} %bitcast.place_ref, s32[64,64]{1,0:T(8,128)} %mask_ref.1, bf16[32,8,128,128]{3,2,1,0:T(8,128)(2,1)} %get-tuple-element.14.x_far, ...), custom_call_target="tpu_custom_call" | custom-call | tf_op jit(solution)/shard_map/attention/pallas_call | solution.py:272
  107.4 0.0 copy-start.2
  107.4 0.0 copy-start.3
  107.5 0.0 copy-start
  107.5 57.6 %reduce.2 = (bf16[2,8,64,128]{3,2,1,0:T(8,128)(2,1)}, bf16[2,32,1,32,256]{4,3,2,1,0:T(8,128)(2,1)}, bf16[8,64,128]{2,1,0:T(8,128)(2,1)}, bf16[8,64,128]{2,1,0:T(8,128)(2,1)}) custom-call(bf16[32,2,8,64,128]{4,3,2,1,0:T(8,128)(2,1)} %bitcast.30, bf16[2,4,32,32,256]{4,3,2,1,0:T(8,128)(2,1)} %bitcast.31, bf16[2,8,64,128]{3,2,1,0:T(8,128)(2,1)} %get-tuple-element.17.out_ref, ...), custom_call_target="tpu_custom_call" | custom-call | tf_op jit(solution)/shard_map/reduce/pallas_call | solution.py:721
  165.1 0.0 copy-done.2
  165.1 0.0 copy-done.3
  165.1 0.9 pad_maximum_fusion.1
  166.1 0.7 copy.27
  166.8 1.2 fusion.10
  168.0 0.1 div.17
  168.1 0.0 copy-done
  168.1 0.5 fusion.5
  168.6 1.3 fusion.8
  170.0 4.7 %layout.1 = f32[32,4,4096]{2,1,0:T(4,128)} custom-call(bf16[2,32,32,256]{3,2,1,0:T(8,128)(2,1)} %bitcast.36), custom_call_target="tpu_custom_call" | custom-call | tf_op jit(solution)/shard_map/layout/pallas_call | solution.py:768
  (8 shorter events, 0.1 us)
Async XLA Ops:
  6.0 2.8 %copy-start.1 = (bf16[8,2,64,128]{3,2,0,1:T(8,128)(2,1)}, bf16[8,2,64,128]{3,2,0,1:T(8,128)(2,1)S(1)}, u32[]{:S(2)}) copy-start(bf16[8,2,64,128]{3,2,0,1:T(8,128)(2,1)S(1)} %copy.31) | copy-start | bytes 786436
  107.4 57.6 %copy-start.2 = (bf16[2,8,64,128]{3,2,1,0:T(8,128)(2,1)S(1)}, bf16[2,8,64,128]{3,2,1,0:T(8,128)(2,1)}, u32[]{:S(2)}) copy-start(bf16[2,8,64,128]{3,2,1,0:T(8,128)(2,1)} %get-tuple-element.17.out_ref) | copy-start | bytes 786436
  107.4 57.6 %copy-start.3 = (bf16[2,8,64,128]{3,2,1,0:T(8,128)(2,1)S(1)}, bf16[2,8,64,128]{3,2,1,0:T(8,128)(2,1)}, u32[]{:S(2)}) copy-start(bf16[2,8,64,128]{3,2,1,0:T(8,128)(2,1)} %get-tuple-element.20.dn_ref) | copy-start | bytes 786436
  107.5 60.7 %copy-start = (bf16[8,128,128]{2,1,0:T(8,128)(2,1)S(1)}, bf16[8,128,128]{2,1,0:T(8,128)(2,1)}, u32[]{:S(2)}) copy-start(bf16[8,128,128]{2,1,0:T(8,128)(2,1)} %param.6) | copy-start | bytes 786436

commit v5 on v4

--- a/solution.py
+++ b/solution.py
@@ -45,7 +45,7 @@
 
 
 def attention_kernel(
-    place_ref, mask_ref, x_far, bias_far, d_out_ref, w_proj_ref, w_out_ref,
+    place_ref, mask_ref, x_far, bias_far, d_out_ref, d_odd_ref, w_proj_ref, w_out_ref,
     out_ref, dn_ref, pair_far, bias_grad_far,
     x_ref, bias_ref, pair_ref, bias_grad_ref, x_sem, move_sem,
     k_ref, v_ref, q_ref, do_ref, bias_f, grad_f, max_ref, sum_ref, delta_ref, acc_ref,
@@ -122,7 +122,8 @@
         x_q = x_q.reshape(rows * TILE, -1)
         queries = (nn(x_q, w_q) * q_scale).astype(BF16)
         gating = jax.nn.sigmoid(nn(x_q, w_gate))
-        d_gated = nt(d_out_ref[a].reshape(rows * TILE, -1), w_out_ref[...])
+        d_out = d_out_ref[:, :TILE] if a == 0 else d_odd_ref[...]
+        d_gated = nt(d_out.reshape(rows * TILE, -1), w_out_ref[...])
         d_att = (d_gated * gating).astype(BF16)
         gate_ref[a] = gating.reshape(rows, TILE, width)
         dg_ref[a] = d_gated.reshape(rows, TILE, width)
@@ -262,7 +263,7 @@
         move.wait()
 
 
-def attention(place, mask, x_all, bias_t, d_out, w_proj, w_out):
+def attention(place, mask, x_all, bias_t, d_out, d_odd, w_proj, w_out):
     blocks, rows, cols, chans = x_all.shape
     tiles = blocks * cols // TILE
     width = H * DH
@@ -277,7 +278,7 @@
             jax.ShapeDtypeStruct((tiles, rows, TILE, chans), BF16),
             jax.ShapeDtypeStruct((2, tiles, TILE, HJ), BF16),
         ),
-        in_specs=[smem, smem, anywhere, anywhere, vmem, vmem, vmem],
+        in_specs=[smem, smem, anywhere, anywhere, vmem, vmem, vmem, vmem],
         out_specs=(vmem, vmem, anywhere, anywhere),
         scratch_shapes=[
             pltpu.VMEM(x_all.shape, BF16),
@@ -304,7 +305,7 @@
         ],
         compiler_params=pltpu.CompilerParams(vmem_limit_bytes=62 * 1024 * 1024),
         name="attention",
-    )(place, mask, x_all, bias_t, d_out, w_proj, w_out)
+    )(place, mask, x_all, bias_t, d_out, d_odd, w_proj, w_out)
 
 
 MESH = pl.DeviceIdType.MESH
@@ -374,20 +375,38 @@
     others += [place.along_x(1), place.along_x(-1), place.sibling(), place.partner()]
     for other in others:
         pl.semaphore_signal(barrier, inc=1, device_id=other, device_id_type=MESH)
-    pl.semaphore_wait(barrier, len(others))
+    return lambda: pl.semaphore_wait(barrier, len(others))
+
+
+def normalize(entries):
+    centred = entries - jnp.mean(entries, axis=-1, keepdims=True)
+    spread = jnp.mean(centred * centred, axis=-1, keepdims=True)
+    scale = lax.rsqrt(spread + eps_norm)
+    return centred * scale, scale
 
 
 def pair_steps(axis, first, second):
     return (first, second) if axis == 0 else (second, first)
 
 
-def gather_kernel(x_ref, bias_ref, d_ref, x_all, bias_all, d_odd, local_sem, send_sem, recv_sem):
+def gather_kernel(
+    slab_ref, bias_in, d_ref, x_all, bias_all, d_odd, x_ref, bias_ref, local_sem, send_sem, recv_sem
+):
     place = Place()
     links = Links(send_sem, recv_sem)
     links.me = place.sibling()
-    greet(place)
+    everyone_here = greet(place)
     rows = x_ref.shape[0]
     half = rows // 2
+
+    def turn_bias(a):
+        step = 2 * TILE
+        for start in range(0, bias_ref.shape[1], step):
+            heads = [bias_in[h, a * TILE : (a + 1) * TILE, start : start + step] for h in range(H)]
+            bias_ref[a, start : start + step, :] = jnp.transpose(jnp.concatenate(heads, axis=0))
+
+    turn_bias(1)
+    everyone_here()
     sub = half // 2
     long = bias_ref.shape[1]
     row = place.row
@@ -401,22 +420,24 @@
     def bias_spot(a, step, start=0, size=None):
         return bias_all.at[a, (row + step) % RING, pl.ds(start, long if size is None else size)]
 
+    odd = links.send(bias_ref.at[1], bias_spot(1, 0), place.partner())
+    for r in range(rows):
+        x_ref[r] = normalize(slab_ref[r].astype(F32))[0].astype(BF16)
+    first = {}
+    for hf in range(2):
+        mine = own(hf * half, half)
+        for step in (1, -1):
+            first[hf, step] = links.send(mine, spot((0, 0), hf * half, half), place.along(hf, step))
+    turn_bias(0)
+    bias_direct = {}
+    for step in (1, -1):
+        bias_direct[0, step] = links.send(bias_ref.at[0], bias_spot(0, 0), place.along_x(step))
     locals_ = [
         pltpu.make_async_copy(x_ref, x_all.at[place.col], local_sem.at[0]),
         pltpu.make_async_copy(bias_ref.at[0], bias_spot(0, 0), local_sem.at[1]),
     ]
     for copy in locals_:
         copy.start()
-
-    odd = links.send(bias_ref.at[1], bias_spot(1, 0), place.partner())
-    bias_direct = {}
-    for step in (1, -1):
-        bias_direct[0, step] = links.send(bias_ref.at[0], bias_spot(0, 0), place.along_x(step))
-    first = {}
-    for hf in range(2):
-        mine = own(hf * half, half)
-        for step in (1, -1):
-            first[hf, step] = links.send(mine, spot((0, 0), hf * half, half), place.along(hf, step))
     second = {}
     chip = {}
 
@@ -440,7 +461,7 @@
 
     for hf in range(2):
         pass_on(hf, 0, own(hf * half, half))
-    d_move = links.send(d_ref.at[1], d_odd, place.partner())
+    d_move = links.send(d_ref.at[:, pl.ds(TILE, TILE)], d_odd, place.partner())
 
     onward = {}
     for step in (1, -1):
@@ -492,27 +513,33 @@
         copy.wait()
 
 
-def gather(normed, bias_pair, d_out_pair):
-    rows, cols, chans = normed.shape
+def gather(pair_slab, pair_bias, d_out):
+    rows, cols, chans = pair_slab.shape
+    keys = pair_bias.shape[2]
     anywhere = pl.BlockSpec(memory_space=pl.ANY)
+    vmem = pl.BlockSpec(memory_space=pltpu.VMEM)
     copies = 100
     return pl.pallas_call(
         gather_kernel,
         out_shape=(
             jax.ShapeDtypeStruct((8 * RING, rows, cols, chans), BF16),
-            jax.ShapeDtypeStruct((2, RING) + bias_pair.shape[1:], BF16),
-            jax.ShapeDtypeStruct(d_out_pair.shape[1:], BF16),
+            jax.ShapeDtypeStruct((2, RING, keys, HJ), BF16),
+            jax.ShapeDtypeStruct((rows, TILE, chans), BF16),
         ),
-        in_specs=[anywhere] * 3,
+        in_specs=[vmem, vmem, anywhere],
         out_specs=(anywhere,) * 3,
         scratch_shapes=[
+            pltpu.VMEM(pair_slab.shape, BF16),
+            pltpu.VMEM((2, keys, HJ), BF16),
             pltpu.SemaphoreType.DMA((2,)),
             pltpu.SemaphoreType.DMA((copies,)),
             pltpu.SemaphoreType.DMA((copies,)),
         ],
-        compiler_params=pltpu.CompilerParams(collective_id=0, has_side_effects=True),
+        compiler_params=pltpu.CompilerParams(
+            collective_id=0, has_side_effects=True, vmem_limit_bytes=62 * 1024 * 1024
+        ),
         name="gather",
-    )(normed, bias_pair, d_out_pair)
+    )(pair_slab, pair_bias, d_out)
 
 
 def add_into(dst, *sources):
@@ -751,62 +778,58 @@
     )(pair, grads, out, dn)
 
 
-def layout_kernel(grad_ref, out_ref):
+def finish_kernel(
+    slab_ref, out_ref, out_odd_ref, dn_ref, dn_odd_ref, pair_ref, grad_ref,
+    attn_ref, slab_grad_ref, bias_grad_ref,
+):
     count = grad_ref.shape[1]
+    rows = slab_ref.shape[0]
     for m in range(count):
         even = grad_ref[0, m].astype(F32)
         odd = grad_ref[1, count - 1 - m].astype(F32)
         for h in range(H):
             part = slice(h * TILE, (h + 1) * TILE)
             both = jnp.concatenate([even[:, part], odd[:, part]], axis=1)
-            out_ref[:, h, 2 * TILE * m : 2 * TILE * (m + 1)] = both
-
-
-def layout(grads):
+            bias_grad_ref[:, h, 2 * TILE * m : 2 * TILE * (m + 1)] = both
+    for r in range(rows):
+        for a in range(2):
+            part = slice(a * TILE, (a + 1) * TILE)
+            attn_ref[r, part] = out_ref[0, r] if a == 0 else out_odd_ref[r]
+            d_own = dn_ref[0, r] if a == 0 else dn_odd_ref[r]
+            d_normed = d_own.astype(F32) + pair_ref[a, r].astype(F32)
+            normed, scale = normalize(slab_ref[r, part].astype(F32))
+            d_mean = jnp.mean(d_normed, axis=-1, keepdims=True)
+            d_along = jnp.mean(d_normed * normed, axis=-1, keepdims=True)
+            slab_grad_ref[r, part] = (scale * (d_normed - d_mean - normed * d_along)).astype(BF16)
+
+
+def finish(pair_slab, out, out_odd, dn, dn_odd, pair_sum, grads):
     count, keys = grads.shape[1:3]
     vmem = pl.BlockSpec(memory_space=pltpu.VMEM)
     return pl.pallas_call(
-        layout_kernel,
-        out_shape=jax.ShapeDtypeStruct((keys, H, 2 * TILE * count), F32),
-        in_specs=[vmem],
-        out_specs=vmem,
-        name="layout",
-    )(grads)
+        finish_kernel,
+        out_shape=(
+            jax.ShapeDtypeStruct(pair_slab.shape, BF16),
+            jax.ShapeDtypeStruct(pair_slab.shape, BF16),
+            jax.ShapeDtypeStruct((keys, H, 2 * TILE * count), F32),
+        ),
+        in_specs=[vmem] * 7,
+        out_specs=(vmem,) * 3,
+        compiler_params=pltpu.CompilerParams(vmem_limit_bytes=62 * 1024 * 1024),
+        name="finish",
+    )(pair_slab, out, out_odd, dn, dn_odd, pair_sum, grads)
 
 
 def on_device(pair_slab, pair_bias, tile_mask, w_proj, w_out, d_out):
-    rows, cols, chans = pair_slab.shape
     ncol = lax.axis_size("col")
     c = lax.axis_index("col")
-    entries = pair_slab.astype(F32)
-    centred = entries - jnp.mean(entries, axis=-1, keepdims=True)
-    spread = jnp.mean(centred * centred, axis=-1, keepdims=True)
-    rstd = lax.rsqrt(spread + eps_norm)
-    normed_f = centred * rstd
-    normed = normed_f.astype(BF16)
-
-    halves = pair_bias.reshape(H, 2, TILE, -1).transpose(1, 3, 0, 2).reshape(2, -1, HJ)
-    d_out_h = d_out.reshape(rows, 2, TILE, chans).transpose(1, 0, 2, 3)
-    x_all, bias_all, d_odd = gather(normed, halves, d_out_h)
+    x_all, bias_all, d_odd = gather(pair_slab, pair_bias, d_out)
     bias_t = bias_all.reshape(2, -1, TILE, HJ)
-    d_out_pair = jnp.stack([d_out_h[0], d_odd])
-
     out, dn, pair, bias_grad = attention(
-        c.reshape(1).astype(jnp.int32), tile_mask, x_all, bias_t, d_out_pair, w_proj, w_out
+        c.reshape(1).astype(jnp.int32), tile_mask, x_all, bias_t, d_out, d_odd, w_proj, w_out
     )
-
     pair_sum, grads, out_odd, dn_odd = reduce(pair, bias_grad, out, dn)
-    attn_out = jnp.stack([out[0], out_odd], axis=1).reshape(rows, cols, chans)
-    dn_own = jnp.stack([dn[0], dn_odd], axis=1).reshape(rows, cols, chans).astype(F32)
-    pair_sum = pair_sum.transpose(1, 0, 2, 3).reshape(rows, cols, chans)
-    d_normed = dn_own + pair_sum.astype(F32)
-    slab_grads = rstd * (
-        d_normed
-        - jnp.mean(d_normed, axis=-1, keepdims=True)
-        - normed_f * jnp.mean(d_normed * normed_f, axis=-1, keepdims=True)
-    )
-    bias_grads = layout(grads.reshape(2, ncol, -1, HJ))
-    return attn_out, slab_grads.astype(BF16), bias_grads
+    return finish(pair_slab, out, out_odd, dn, dn_odd, pair_sum, grads.reshape(2, ncol, -1, HJ))
 
 
 def solution(mesh):

time: 175 us -> 165 us (0.943)
  other arithmetic: 10 us -> 0 us
  Pallas kernels: 159 us -> 164 us
  local copies, waits for them, and re-layouts: 4.58 us -> 0 us
    reduce_sum x4 -> x0, other arithmetic: 4.1 us -> none  [the longest x1 1.32 us: on_device(): spread = jnp.mean(centred * centred, axis=-1, keepdims=True)]
    convert_element_type x2 -> x0, other arithmetic: 3.31 us -> none  [the longest x1 1.99 us: on_device(): normed = normed_f.astype(BF16)]
    pallas_call x1, Pallas kernels: 4.68 us -> 7.53 us  [finish(): pl.pallas_call(finish_kernel, out_shape=(jax.ShapeDtypeStruct(pair_slab.s...]
    another operation x2 -> x0, other arithmetic: 2.56 us -> none  [the longest x1 1.63 us: on_device(): d_out_pair = jnp.stack([d_out_h[0], d_odd])]
    reshape x2 -> x0, local copies, waits for them, and re-layouts: 2.28 us -> none  [the longest x1 1.31 us: on_device(): pair_bias.reshape(H, 2, TILE, -1).transpose(1, 3, 0, 2).reshape(2, -1, HJ)]
where the time goes in v5:
time: 165 us; the launch traced here: 164 us
  Pallas kernels  164 us (99%)
    pallas_call x1, Pallas kernels, reduce(): pl.pallas_call(reduce_kernel, out_shape=(jax.ShapeDtypeStruct((2,) + bloc...  58.3 us
    pallas_call x1, Pallas kernels, gather(): pl.pallas_call(gather_kernel, out_shape=(jax.ShapeDtypeStruct((8 * RING,...  51.8 us
    pallas_call x1, Pallas kernels, attention(): pl.pallas_call(attention_kernel, out_shape=(jax.ShapeDtypeStruct((2, rows...  46.2 us
    pallas_call x1, Pallas kernels, finish(): pl.pallas_call(finish_kernel, out_shape=(jax.ShapeDtypeStruct(pair_slab.s...  7.53 us

profile of v5, /device:TPU:1, one launch (start us, length us, event | category | flops | bytes accessed | tf_op | source)
XLA Modules:
  0.0 164.5 jit_solution(17889540080701336982)
XLA Ops:
  0.6 51.8 %gather.1 = (bf16[32,8,128,128]{3,2,1,0:T(8,128)(2,1)}, bf16[2,4,1024,256]{3,2,1,0:T(8,128)(2,1)}, bf16[8,64,128]{2,1,0:T(8,128)(2,1)}) custom-call(bf16[8,128,128]{2,1,0:T(8,128)(2,1)} %slab_ref.3, bf16[4,128,1024]{2,1,0:T(8,128)(2,1)} %bias_in.1, bf16[8,128,128]{2,1,0:T(8,128)(2,1)} %d_out_ref.1), custom_call_target="tpu_custom_call" | custom-call | tf_op jit(solution)/shard_map/gather/pallas_call | solution.py:522
  52.4 46.2 %attention.1 = (bf16[2,8,64,128]{3,2,1,0:T(8,128)(2,1)}, bf16[2,8,64,128]{3,2,1,0:T(8,128)(2,1)}, bf16[64,8,64,128]{3,2,1,0:T(8,128)(2,1)}, bf16[2,64,64,256]{3,2,1,0:T(8,128)(2,1)}) custom-call(s32[1]{0:T(128)} %bitcast.place_ref, s32[64,64]{1,0:T(8,128)} %mask_ref.1, bf16[32,8,128,128]{3,2,1,0:T(8,128)(2,1)} %get-tuple-element.14.x_far, ...), custom_call_target="tpu_custom_call" | custom-call | tf_op jit(solution)/shard_map/attention/pallas_call | solution.py:273
  98.7 58.3 %reduce.1 = (bf16[2,8,64,128]{3,2,1,0:T(8,128)(2,1)}, bf16[2,32,1,32,256]{4,3,2,1,0:T(8,128)(2,1)}, bf16[8,64,128]{2,1,0:T(8,128)(2,1)}, bf16[8,64,128]{2,1,0:T(8,128)(2,1)}) custom-call(bf16[32,2,8,64,128]{4,3,2,1,0:T(8,128)(2,1)} %bitcast.5, bf16[2,4,32,32,256]{4,3,2,1,0:T(8,128)(2,1)} %bitcast.6, bf16[2,8,64,128]{3,2,1,0:T(8,128)(2,1)} %get-tuple-element.17.out_ref, ...), custom_call_target="tpu_custom_call" | custom-call | tf_op jit(solution)/shard_map/reduce/pallas_call | solution.py:748
  157.0 7.5 %finish.1 = (bf16[8,128,128]{2,1,0:T(8,128)(2,1)}, bf16[8,128,128]{2,1,0:T(8,128)(2,1)}, f32[32,4,4096]{2,1,0:T(4,128)}) custom-call(bf16[8,128,128]{2,1,0:T(8,128)(2,1)} %slab_ref.3, bf16[2,8,64,128]{3,2,1,0:T(8,128)(2,1)} %get-tuple-element.17.out_ref, bf16[8,64,128]{2,1,0:T(8,128)(2,1)} %get-tuple-element.21.out_odd_ref, ...), custom_call_target="tpu_custom_call" | custom-call | tf_op jit(solution)/shard_map/finish/pallas_call | solution.py:809

commit v6 on v5

--- a/solution.py
+++ b/solution.py
@@ -805,16 +805,27 @@
 
 def finish(pair_slab, out, out_odd, dn, dn_odd, pair_sum, grads):
     count, keys = grads.shape[1:3]
-    vmem = pl.BlockSpec(memory_space=pltpu.VMEM)
+    rows, cols, chans = pair_slab.shape
+    parts = 2
+    whole = pl.BlockSpec((rows // parts, cols, chans), lambda i: (i, 0, 0))
+    odd = pl.BlockSpec((rows // parts, TILE, chans), lambda i: (i, 0, 0))
+    both = pl.BlockSpec((2, rows // parts, TILE, chans), lambda i: (0, i, 0, 0))
     return pl.pallas_call(
         finish_kernel,
+        grid=(parts,),
         out_shape=(
             jax.ShapeDtypeStruct(pair_slab.shape, BF16),
             jax.ShapeDtypeStruct(pair_slab.shape, BF16),
             jax.ShapeDtypeStruct((keys, H, 2 * TILE * count), F32),
         ),
-        in_specs=[vmem] * 7,
-        out_specs=(vmem,) * 3,
+        in_specs=[
+            whole, both, odd, both, odd, both,
+            pl.BlockSpec((2, count, keys // parts, HJ), lambda i: (0, 0, i, 0)),
+        ],
+        out_specs=(
+            whole, whole,
+            pl.BlockSpec((keys // parts, H, 2 * TILE * count), lambda i: (i, 0, 0)),
+        ),
         compiler_params=pltpu.CompilerParams(vmem_limit_bytes=62 * 1024 * 1024),
         name="finish",
     )(pair_slab, out, out_odd, dn, dn_odd, pair_sum, grads)

time: 165 us -> 165 us (level)
  no operation moved by 1% of the time
where the time goes in v6:
time: 165 us; the launch traced here: 164 us
  Pallas kernels  164 us (99%)
    pallas_call x1, Pallas kernels, reduce(): pl.pallas_call(reduce_kernel, out_shape=(jax.ShapeDtypeStruct((2,) + bloc...  59.6 us
    pallas_call x1, Pallas kernels, gather(): pl.pallas_call(gather_kernel, out_shape=(jax.ShapeDtypeStruct((8 * RING,...  51.8 us
    pallas_call x1, Pallas kernels, attention(): pl.pallas_call(attention_kernel, out_shape=(jax.ShapeDtypeStruct((2, rows...  46.2 us
    pallas_call x1, Pallas kernels, finish(): pl.pallas_call(finish_kernel, grid=(parts,), out_shape=(jax.ShapeDtypeStr...  6.12 us

profile of v6, /device:TPU:1, one launch (start us, length us, event | category | flops | bytes accessed | tf_op | source)
XLA Modules:
  0.0 164.4 jit_solution(10315487635053374873)
XLA Ops:
  0.6 51.8 %gather.1 = (bf16[32,8,128,128]{3,2,1,0:T(8,128)(2,1)}, bf16[2,4,1024,256]{3,2,1,0:T(8,128)(2,1)}, bf16[8,64,128]{2,1,0:T(8,128)(2,1)}) custom-call(bf16[8,128,128]{2,1,0:T(8,128)(2,1)} %slab_ref.3, bf16[4,128,1024]{2,1,0:T(8,128)(2,1)} %bias_in.1, bf16[8,128,128]{2,1,0:T(8,128)(2,1)} %d_out_ref.1), custom_call_target="tpu_custom_call" | custom-call | tf_op jit(solution)/shard_map/gather/pallas_call | solution.py:522
  52.4 46.2 %attention.1 = (bf16[2,8,64,128]{3,2,1,0:T(8,128)(2,1)}, bf16[2,8,64,128]{3,2,1,0:T(8,128)(2,1)}, bf16[64,8,64,128]{3,2,1,0:T(8,128)(2,1)}, bf16[2,64,64,256]{3,2,1,0:T(8,128)(2,1)}) custom-call(s32[1]{0:T(128)} %bitcast.place_ref, s32[64,64]{1,0:T(8,128)} %mask_ref.1, bf16[32,8,128,128]{3,2,1,0:T(8,128)(2,1)} %get-tuple-element.14.x_far, ...), custom_call_target="tpu_custom_call" | custom-call | tf_op jit(solution)/shard_map/attention/pallas_call | solution.py:273
  98.7 59.6 %reduce.1 = (bf16[2,8,64,128]{3,2,1,0:T(8,128)(2,1)}, bf16[2,32,1,32,256]{4,3,2,1,0:T(8,128)(2,1)}, bf16[8,64,128]{2,1,0:T(8,128)(2,1)}, bf16[8,64,128]{2,1,0:T(8,128)(2,1)}) custom-call(bf16[32,2,8,64,128]{4,3,2,1,0:T(8,128)(2,1)} %bitcast.5, bf16[2,4,32,32,256]{4,3,2,1,0:T(8,128)(2,1)} %bitcast.6, bf16[2,8,64,128]{3,2,1,0:T(8,128)(2,1)} %get-tuple-element.17.out_ref, ...), custom_call_target="tpu_custom_call" | custom-call | tf_op jit(solution)/shard_map/reduce/pallas_call | solution.py:748
  158.2 6.1 %finish.1 = (bf16[8,128,128]{2,1,0:T(8,128)(2,1)}, bf16[8,128,128]{2,1,0:T(8,128)(2,1)}, f32[32,4,4096]{2,1,0:T(4,128)}) custom-call(bf16[8,128,128]{2,1,0:T(8,128)(2,1)} %slab_ref.3, bf16[2,8,64,128]{3,2,1,0:T(8,128)(2,1)} %get-tuple-element.17.out_ref, bf16[8,64,128]{2,1,0:T(8,128)(2,1)} %get-tuple-element.21.out_odd_ref, ...), custom_call_target="tpu_custom_call" | custom-call | tf_op jit(solution)/shard_map/finish/pallas_call | solution.py:813
